TPU v7x, 1024 devices: a whole 4x4x32 slice. The times are simulated.
1024 devices in a mesh: replica: 16 (over x, y), owner: 64 (over z, core).
Axes of the slice: x: 4, y: 4, z: 32, core: 2. Of those that a mesh axis runs over, the one named last changes fastest.
Arguments:
- grad_parts: bfloat16 [16, 96, 512, 512], P('replica', None, 'owner'), may hold values from -1.5 to 1.5
- block_owner: int32 [96], replicated, may hold values from 0 to 63, as said below
- left_basis: float32 [128, 512, 512], P('owner'), may hold values from -0.25 to 0.25
- right_basis: float32 [128, 512, 512], P('owner'), may hold values from -0.25 to 0.25
- first_moment: bfloat16 [128, 512, 512], P('owner'), may hold values from -0.59765625 to 0.59765625
- second_moment: bfloat16 [128, 512, 512], P('owner'), may hold values from 0.0099487305 to 0.099609375
Outputs:
- direction: bfloat16 [96, 512, 512], P(None, 'owner')
- new_first: bfloat16 [128, 512, 512], P('owner')
- new_second: bfloat16 [128, 512, 512], P('owner')
Inputs may be any that keep to these rules, and one draw needn't show every extreme that they name: `block_owner`: every owner is named by one or two blocks (at most 2).
All inputs are finite; a program needn't handle non-finite values.
Results may differ from a plain program's by a relative error of at most 0.024.
Values may be sent and summed in bfloat16 or wider, within the bound.
No kernel may reach another device: no remote copies, remote signals or barrier semaphores. Data moves between devices by JAX's collectives and lax.ppermute only.
A program may use at most 32 MiB of HBM per device.

v0:
```python
import jax
import jax.numpy as jnp
from jax import lax
from jax.sharding import PartitionSpec as P

beta_first = 0.9
beta_second = 0.95
bias_first = 1.0 - 0.9**20
bias_second = 1.0 - 0.95**20
epsilon = 1e-08


def local(grad_parts, block_owner, left_basis, right_basis, first_moment, second_moment):
    owners = lax.axis_size("owner")
    strips = grad_parts[0]
    count = strips.shape[0]
    rows = strips.shape[1]
    width = strips.shape[2]
    levels_here = left_basis.shape[0]
    index = jnp.arange(count, dtype=jnp.int32)
    same = block_owner[:, None] == block_owner[None, :]
    earlier = index[None, :] < index[:, None]
    level = jnp.sum((same & earlier).astype(jnp.int32), axis=1)
    owner_hit = block_owner[:, None, None] == jnp.arange(owners, dtype=jnp.int32)[None, :, None]
    level_hit = level[:, None, None] == jnp.arange(levels_here, dtype=jnp.int32)[None, None, :]
    picker = (owner_hit & level_hit).astype(jnp.bfloat16)
    placed = jnp.einsum("bol,brc->lorc", picker, strips, preferred_element_type=jnp.float32)
    moved = lax.all_to_all(
        placed.astype(jnp.bfloat16).reshape(levels_here, owners * rows, width),
        "owner",
        split_axis=1,
        concat_axis=1,
        tiled=True,
    )
    summed = lax.psum(moved.astype(jnp.float32).astype(jnp.bfloat16), "replica")
    rotated = jnp.einsum(
        "sji,sjk->sik", left_basis, summed.astype(jnp.float32), precision=lax.Precision.HIGHEST
    )
    rotated = jnp.einsum("sik,skl->sil", rotated, right_basis, precision=lax.Precision.HIGHEST)
    first = beta_first * first_moment.astype(jnp.float32) + (1.0 - beta_first) * rotated
    second = (
        beta_second * second_moment.astype(jnp.float32) + (1.0 - beta_second) * rotated * rotated
    )
    update = (first / bias_first / (jnp.sqrt(second / bias_second) + epsilon)).astype(jnp.bfloat16)
    left_half = jnp.einsum(
        "sij,sjk->sik", left_basis.astype(jnp.bfloat16), update, preferred_element_type=jnp.float32
    ).astype(jnp.bfloat16)
    slot_dir = jnp.einsum(
        "sik,slk->sil",
        left_half,
        right_basis.astype(jnp.bfloat16),
        preferred_element_type=jnp.float32,
    ).astype(jnp.bfloat16)
    returned = lax.all_to_all(slot_dir, "owner", split_axis=1, concat_axis=1, tiled=True)
    returned = returned.reshape(levels_here, owners, rows, width)
    direction = jnp.einsum(
        "bol,lorc->brc", picker, returned, preferred_element_type=jnp.float32
    ).astype(jnp.bfloat16)
    return (direction, first.astype(jnp.bfloat16), second.astype(jnp.bfloat16))


def solution(mesh):
    return jax.shard_map(
        local,
        mesh=mesh,
        in_specs=(
            P("replica", None, "owner", None),
            P(),
            P("owner", None, None),
            P("owner", None, None),
            P("owner", None, None),
            P("owner", None, None),
        ),
        out_specs=(P(None, "owner", None), P("owner", None, None), P("owner", None, None)),
        check_vma=False,
    )
```

profile of v0, /device:TPU:2, one launch (start us, length us, event | category | flops | bytes accessed | tf_op | source)
XLA Modules:
  0.0 456.0 jit_solution(11584891621783757893)
XLA Ops:
  7.2 0.0 all-reduce.2.cloned.1.call-start
  7.2 0.9 convert_reduce_fusion
  8.1 0.7 iota_compare_fusion.1
  8.8 1.7 fusion.1
  10.5 0.6 copy.61
  11.1 1.1 copy.38
  12.2 139.8 %all_to_all.10 = bf16[2,512,512]{2,0,1:T(2,128)(2,1)S(1)} all-to-all(bf16[2,512,512]{2,0,1:T(2,128)(2,1)S(1)} %copy.38), channel_id=1, replica_groups=mesh['replica'=16,'owner'=64] {'owner'}, dimensions={1} | all-to-all | bytes 2097152 | tf_op jit(solution)/shard_map/all_to_all | solution.py:28
  152.1 2.5 copy.39
  154.5 0.0 all-reduce.2.cloned.1.call-update
  154.6 0.0 copy-start
  154.6 0.0 copy-start.1
  154.6 139.8 %all-reduce.2.cloned.1.call-done = bf16[2,512,512]{1,2,0:T(8,128)(2,1)} async-done(((bf16[2,512,512]{1,2,0:T(8,128)(2,1)}), bf16[2,512,512]{1,2,0:T(8,128)(2,1)}) %all-reduce.2.cloned.1.call-update) | async-done | bytes 1048592 | tf_op jit(solution)/shard_map/psum | solution.py:35
  294.4 0.0 copy-start.2
  294.4 3.8 fusion.41
  298.3 0.0 copy-done
  298.3 0.0 copy-done.1
  298.3 0.0 copy-done.2
  298.3 5.4 %fusion.3 = (bf16[2,512,512]{2,1,0:T(8,128)(2,1)}, bf16[2,512,512]{2,1,0:T(8,128)(2,1)}, f32[2,512,512]{2,1,0:T(8,128)}) fusion(bf16[2,512,512]{2,1,0:T(8,128)(2,1)S(1)} %copy-done.1, bf16[2,512,512]{2,1,0:T(8,128)(2,1)S(1)} %copy-done.2, f32[2,512,512]{1,2,0:T(8,128)S(1)} %fusion.41, f32[2,512,512]{2,1,0:T(8,128)S(1)} %copy-done), kind=kOutput, calls=%fused_computation.10 | convolution fusion | flops 3226992640 | bytes 10485760 | tf_op jit(solution)/shard_map/sik,skl->sil/dot_general | solution.py:39
  303.7 6.4 %convolution_convert_fusion = bf16[2,512,512]{2,1,0:T(8,128)(2,1)} fusion(f32[2,512,512]{2,1,0:T(8,128)S(1)} %copy-done, f32[2,512,512]{2,1,0:T(8,128)} %param.8, f32[2,512,512]{2,1,0:T(8,128)} %get-tuple-element.20, bf16[2,512,512]{2,1,0:T(8,128)(2,1)} %param.10, bf16[2,512,512]{2,1,0:T(8,128)(2,1)S(1)} %copy-done.1), kind=kOutput, calls=%fused_computation.5 | convolution fusion | flops 1083179008 | bytes 9437184 | tf_op jit(solution)/shard_map/sik,slk->sil/dot_general | solution.py:48
  310.2 2.3 copy.43
  312.5 134.0 %all_to_all.11 = bf16[2,512,512]{2,0,1:T(2,128)(2,1)S(1)} all-to-all(bf16[2,512,512]{2,0,1:T(2,128)(2,1)S(1)} %copy.43), channel_id=1, replica_groups=mesh['replica'=16,'owner'=64] {'owner'}, dimensions={1} | all-to-all | bytes 2097152 | tf_op jit(solution)/shard_map/all_to_all | solution.py:54
  446.5 1.3 bitcast_convert_fusion
  447.8 1.3 copy.46
  (1 shorter events, 0.0 us)
Async XLA Ops:
  7.2 287.3 %all-reduce.2.cloned.1.call-start = ((), (), s32[]{:S(2)}) async-start(), calls=%async_computation.2 | async-start | bytes 2097152 | tf_op jit(solution)/shard_map/psum | solution.py:35
  154.6 143.7 %copy-start = (f32[2,512,512]{2,1,0:T(8,128)S(1)}, f32[2,512,512]{2,1,0:T(8,128)}, u32[]{:S(2)}) copy-start(f32[2,512,512]{2,1,0:T(8,128)} %param.9) | copy-start | bytes 6291460
  154.6 143.7 %copy-start.1 = (bf16[2,512,512]{2,1,0:T(8,128)(2,1)S(1)}, bf16[2,512,512]{2,1,0:T(8,128)(2,1)}, u32[]{:S(2)}) copy-start(bf16[2,512,512]{2,1,0:T(8,128)(2,1)} %param.11) | copy-start | bytes 3145732
  294.4 3.9 copy-start.2
Sparse Core Ops, SparseCore 0:
  154.7 139.7 all-reduce.1
where the time goes:
time: 456 us
  blocking collectives  274 us (60%)
  waiting for transfers between devices  140 us (31%)
  matrix products  18.7 us (4%)
  between operations  14.1 us (3%)
  local copies, waits for them, and re-layouts  7.77 us (2%)
    psum x1, waiting for transfers between devices, local(): summed = lax.psum(moved.astype(jnp.float32).astype(jnp.bfloat16), 'replica')  140 us
    all_to_all x1, blocking collectives, local(): lax.all_to_all(placed.astype(jnp.bfloat16).reshape(levels_here, owners *...  140 us
    all_to_all x1, blocking collectives, local(): lax.all_to_all(slot_dir, 'owner', split_axis=1, concat_axis=1, tiled=True)  134 us
  transfers between devices with their start and end apart: 1, of which 1 were waited for; matrix products, arithmetic and copies ran while one was open for 0% of the time, Pallas kernels for 0%

commit v1 on v0

v1 whole, which is shorter than its diff:
```python
import functools

import jax
import jax.numpy as jnp
from jax import lax
from jax.experimental import pallas as pl
from jax.experimental.pallas import tpu as pltpu
from jax.sharding import PartitionSpec as P

beta_first = 0.9
beta_second = 0.95
bias_first = 1.0 - 0.9**20
bias_second = 1.0 - 0.95**20
epsilon = 1e-08

PAIRS = 4
TILES = 4
PIECES = PAIRS * TILES
LANES = 128
GROUP = 16

f32 = jnp.float32
bf16 = jnp.bfloat16


def dot(a, b):
    return jnp.dot(a, b, preferred_element_type=f32)


def permutation(dtype):
    out = lax.broadcasted_iota(jnp.int32, (8 * GROUP, 8 * GROUP), 0)
    src = lax.broadcasted_iota(jnp.int32, (8 * GROUP, 8 * GROUP), 1)
    pair = out >> 5
    block = (out & 31) >> 1
    return (src == block * 8 + pair * 2 + (out & 1)).astype(dtype)


def inverse_permutation(dtype):
    out = lax.broadcasted_iota(jnp.int32, (8 * GROUP, 8 * GROUP), 0)
    src = lax.broadcasted_iota(jnp.int32, (8 * GROUP, 8 * GROUP), 1)
    pair = src >> 5
    block = (src & 31) >> 1
    return (out == block * 8 + pair * 2 + (src & 1)).astype(dtype)


def cut_kernel(strips, pieces):
    perm = permutation(bf16)
    for g in range(strips.shape[0] // (8 * GROUP)):
        moved = dot(perm, strips[g * 128 : (g + 1) * 128, :]).astype(bf16)
        for pair in range(PAIRS):
            for tile in range(TILES):
                pieces[pair * TILES + tile, g * 32 : (g + 1) * 32, :] = moved[
                    pair * 32 : (pair + 1) * 32, tile * LANES : (tile + 1) * LANES
                ]


def join_kernel(pieces, strips):
    perm = inverse_permutation(bf16)
    for g in range(strips.shape[0] // (8 * GROUP)):
        rows = [
            jnp.concatenate(
                [pieces[pair * TILES + tile, g * 32 : (g + 1) * 32, :] for tile in range(TILES)],
                axis=1,
            )
            for pair in range(PAIRS)
        ]
        strips[g * 128 : (g + 1) * 128, :] = dot(perm, jnp.concatenate(rows, axis=0)).astype(bf16)


def prep_kernel(owner_col, owner_row, left, right, place, pick, left_p, left_t, right_b, right_t):
    perm = permutation(bf16)
    count2 = owner_row.shape[1]
    col = lax.broadcasted_iota(jnp.int32, (count2, count2), 0) >> 1
    row = lax.broadcasted_iota(jnp.int32, (count2, count2), 1) >> 1
    same = owner_col[...] == owner_row[...]
    level_row = jnp.sum((same & (col < row)).astype(f32), axis=0, keepdims=True) * 0.5
    level_col = jnp.sum((same & (row < col)).astype(f32), axis=1, keepdims=True) * 0.5
    for level in range(2):
        out = lax.broadcasted_iota(jnp.int32, (128, count2), 0)
        src = lax.broadcasted_iota(jnp.int32, (128, count2), 1)
        hit = (owner_row[...] == (out >> 1)) & (level_row == level) & ((out & 1) == (src & 1))
        place[level, :, :] = hit.astype(bf16)
        out = lax.broadcasted_iota(jnp.int32, (count2, 128), 0)
        src = lax.broadcasted_iota(jnp.int32, (count2, 128), 1)
        hit = (owner_col[...] == (src >> 1)) & (level_col == level) & ((out & 1) == (src & 1))
        pick[level, :, :] = hit.astype(bf16)
        parts = [
            dot(perm, left[level, g * 128 : (g + 1) * 128, :].astype(bf16)) for g in range(PAIRS)
        ]
        for pair in range(PAIRS):
            here = jnp.concatenate([part[pair * 32 : (pair + 1) * 32] for part in parts], axis=0)
            left_p[level, pair * 128 : (pair + 1) * 128, :] = here.astype(bf16)
            left_t[level, :, pair * 128 : (pair + 1) * 128] = here.T.astype(bf16)
        right_b[level, :, :] = right[level, :, :].astype(bf16)
        right_t[level, :, :] = right[level, :, :].T.astype(bf16)


def place_kernel(pieces, place, placed):
    total = pieces[0].astype(f32)
    for k in range(1, PIECES):
        total = total + pieces[k].astype(f32)
    total = total.astype(bf16)
    for level in range(2):
        placed[:, level * LANES : (level + 1) * LANES] = dot(place[level], total).astype(bf16)


def step_kernel(
    where, gathered, left_p, left_t, right_b, right_t, first_old, second_old, piece, first_new, second_new
):
    for level in range(2):
        lanes = slice(level * LANES, (level + 1) * LANES)
        grad = jnp.concatenate(
            [
                jnp.concatenate(
                    [gathered[pair * TILES + tile, :, lanes] for tile in range(TILES)], axis=1
                )
                for pair in range(PAIRS)
            ],
            axis=0,
        )
        half = dot(left_t[level], grad).astype(bf16)
        rotated = dot(half, right_b[level])
        first = beta_first * first_old[level].astype(f32) + (1.0 - beta_first) * rotated
        second = (
            beta_second * second_old[level].astype(f32) + (1.0 - beta_second) * rotated * rotated
        )
        first_new[level, :, :] = first.astype(bf16)
        second_new[level, :, :] = second.astype(bf16)
        update = ((first / bias_first) / (jnp.sqrt(second / bias_second) + epsilon)).astype(bf16)
        mine = left_p[level, pl.ds(pl.multiple_of(where[0] * 128, 128), 128), :]
        left_half = dot(mine, update).astype(bf16)
        turned = right_t[level, :, pl.ds(pl.multiple_of(where[1] * LANES, LANES), LANES)]
        piece[:, lanes] = dot(left_half, turned).astype(bf16)


def pick_kernel(returned, pick, copies):
    mine = (dot(pick[0], returned[:, :LANES]) + dot(pick[1], returned[:, LANES:])).astype(bf16)
    for k in range(PIECES):
        copies[k, :, :] = mine


VMEM = pl.BlockSpec(memory_space=pltpu.VMEM)
SMEM = pl.BlockSpec(memory_space=pltpu.SMEM)


def shape(dims, dtype):
    return jax.ShapeDtypeStruct(dims, dtype)


def call(kernel, out, inputs, specs=None, scratch=(), limit=32, cost=None):
    single = not isinstance(out, (list, tuple))
    return pl.pallas_call(
        kernel,
        out_shape=out,
        in_specs=specs or [VMEM] * len(inputs),
        out_specs=VMEM if single else [VMEM] * len(out),
        scratch_shapes=scratch,
        cost_estimate=cost,
        compiler_params=pltpu.CompilerParams(vmem_limit_bytes=limit * 2**20),
    )(*inputs)


def local(grad_parts, block_owner, left_basis, right_basis, first_moment, second_moment):
    count, rows, width = grad_parts.shape[1:]
    replica = lax.axis_index("replica")
    owner2 = jnp.repeat(block_owner, 2)
    strips = grad_parts.reshape(count * rows, width)
    pieces = call(cut_kernel, shape((PIECES, count * 2, LANES), bf16), (strips,))
    parts = lax.all_to_all(pieces, "replica", 0, 0)
    wide = shape((2, width, width), bf16)
    place, pick, left_p, left_t, right_b, right_t = call(
        prep_kernel,
        [shape((2, 128, count * 2), bf16), shape((2, count * 2, 128), bf16), wide, wide, wide, wide],
        (owner2[:, None], owner2[None, :], left_basis, right_basis),
        cost=pl.CostEstimate(flops=4 * 10**9, bytes_accessed=8 * 2**20, transcendentals=0),
    )
    placed = call(place_kernel, shape((128, 2 * LANES), bf16), (parts, place))
    moved = lax.all_to_all(placed.reshape(64, 2, 2 * LANES), "owner", 0, 0).reshape(128, 2 * LANES)
    gathered = lax.all_to_all(
        jnp.broadcast_to(moved[None], (PIECES, 128, 2 * LANES)), "replica", 0, 0
    )
    where = jnp.stack([replica // TILES, replica % TILES]).astype(jnp.int32)
    piece, first, second = call(
        step_kernel,
        [shape((128, 2 * LANES), bf16), wide, wide],
        (where, gathered, left_p, left_t, right_b, right_t, first_moment, second_moment),
        specs=[SMEM] + [VMEM] * 7,
    )
    returned = lax.all_to_all(piece.reshape(64, 2, 2 * LANES), "owner", 0, 0)
    copies = call(
        pick_kernel,
        shape((PIECES, count * 2, LANES), bf16),
        (returned.reshape(128, 2 * LANES), pick),
    )
    joined = lax.all_to_all(copies, "replica", 0, 0)
    direction = call(join_kernel, shape((count * rows, width), bf16), (joined,))
    return direction.reshape(count, rows, width), first, second


def solution(mesh):
    return jax.shard_map(
        local,
        mesh=mesh,
        in_specs=(
            P("replica", None, "owner", None),
            P(),
            P("owner", None, None),
            P("owner", None, None),
            P("owner", None, None),
            P("owner", None, None),
        ),
        out_specs=(P(None, "owner", None), P("owner", None, None), P("owner", None, None)),
        check_vma=False,
    )
```

time: 456 us -> 160 us (0.35)
  the two profiles are of different devices: /device:TPU:2 before, /device:TPU:8 now
where the time goes in v1:
time: 160 us; the launch traced here: 159 us
  blocking collectives  96.3 us (60%)
  starting transfers between devices  21.4 us (13%)
  waiting for transfers between devices  17.2 us (11%)
  local copies, waits for them, and re-layouts  14.6 us (9%)
  Pallas kernels  8.85 us (6%)
    all_to_all x1, blocking collectives, local(): lax.all_to_all(placed.reshape(64, 2, 2 * LANES), 'owner', 0, 0)  49.3 us
    all_to_all x1, blocking collectives, local(): returned = lax.all_to_all(piece.reshape(64, 2, 2 * LANES), 'owner', 0, 0)  30.7 us
    all_to_all x1, starting transfers between devices, local(): parts = lax.all_to_all(pieces, 'replica', 0, 0)  16.5 us
    all_to_all x1, blocking collectives, local(): joined = lax.all_to_all(copies, 'replica', 0, 0)  16.3 us
    all_to_all x1, waiting for transfers between devices, local(): lax.all_to_all(jnp.broadcast_to(moved[None], (PIECES, 128, 2 * LANES)), '...  15.3 us
    unnamed x28, local copies, waits for them, and re-layouts  13.1 us
    pallas_call x6, Pallas kernels, call(): pl.pallas_call(kernel, out_shape=out, in_specs=specs or [VMEM] * len(inpu...  8.85 us
    all_to_all x1, starting transfers between devices, local(): lax.all_to_all(jnp.broadcast_to(moved[None], (PIECES, 128, 2 * LANES)), '...  4.9 us
  transfers between devices with their start and end apart: 2, of which 2 were waited for; matrix products, arithmetic and copies ran while one was open for 0% of the time, Pallas kernels for 1%

profile of v1, /device:TPU:8, one launch (start us, length us, event | category | flops | bytes accessed | tf_op | source)
XLA Modules:
  0.0 159.2 jit_solution(76662510935887811)
XLA Ops:
  0.6 0.0 copy-start.13
  0.6 0.0 copy-start.10
  0.6 1.1 copy-done.10
  1.8 1.2 shard_map.85
  3.0 16.5 %all-to-all-start = ((bf16[16,192,128]{2,1,0:T(8,128)(2,1)}), bf16[16,192,128]{2,1,0:T(8,128)(2,1)S(1)}, u32[]{:S(2)}, u32[]{:S(2)}) async-start(bf16[16,192,128]{2,1,0:T(8,128)(2,1)} %shard_map.85), calls=%async_computation | async-start | bytes 1572864 | tf_op jit(solution)/shard_map/all_to_all | solution.py:169
  19.5 0.0 copy-done.13
  19.5 0.1 broadcast_in_dim.10
  19.6 0.1 broadcast_in_dim_reshape.8.owner_row
  19.7 0.1 broadcast_in_dim_reshape.9.owner_col
  19.8 0.0 copy-start.11
  19.8 1.6 %copy-done.11 = f32[2,512,512]{2,1,0:T(8,128)S(1)} copy-done((f32[2,512,512]{2,1,0:T(8,128)S(1)}, f32[2,512,512]{2,1,0:T(8,128)}, u32[]{:S(2)}) %copy-start.11) | copy-done | bytes 2097176
  21.4 0.0 copy-start.12
  21.4 1.6 copy-done.12
  23.0 1.0 shard_map.86
  24.0 0.0 copy-start.2
  24.0 1.0 copy-done.2
  24.9 0.0 copy-start.4
  24.9 1.0 copy-done.4
  25.9 0.0 copy-start.6
  25.9 1.0 copy-done.6
  26.9 0.0 copy-start.8
  26.9 1.0 copy-done.8
  27.9 1.9 %all-to-all-done.pieces = bf16[16,192,128]{2,1,0:T(8,128)(2,1)S(1)} async-done(((bf16[16,192,128]{2,1,0:T(8,128)(2,1)}), bf16[16,192,128]{2,1,0:T(8,128)(2,1)S(1)}, u32[]{:S(2)}, u32[]{:S(2)}) %all-to-all-start) | async-done | bytes 786464 | tf_op jit(solution)/shard_map/all_to_all | solution.py:169
  29.7 0.0 copy-start
  29.7 0.0 copy-start.1
  29.7 0.3 shard_map.87
  30.0 49.3 %all_to_all.25 = bf16[64,2,256]{2,1,0:T(2,128)(2,1)S(1)} all-to-all(bf16[64,2,256]{2,1,0:T(2,128)(2,1)S(1)} %reshape.23), channel_id=1, replica_groups=mesh['replica'=16,'owner'=64] {'owner'}, dimensions={0} | all-to-all | bytes 131072 | tf_op jit(solution)/shard_map/all_to_all | solution.py:178
  79.4 1.1 broadcast_in_dim.12
  80.5 4.9 %all-to-all-start.2 = ((bf16[16,128,256]{2,1,0:T(8,128)(2,1)}), bf16[16,128,256]{2,1,0:T(8,128)(2,1)S(1)}, u32[]{:S(2)}, u32[]{:S(2)}) async-start(bf16[16,128,256]{2,1,0:T(8,128)(2,1)} %broadcast_in_dim.12), calls=%async_computation.2 | async-start | bytes 2097152 | tf_op jit(solution)/shard_map/all_to_all | solution.py:179
  85.4 0.1 pad_add_fusion.where
  85.5 15.3 %all-to-all-done.2.gathered = bf16[16,128,256]{2,1,0:T(8,128)(2,1)S(1)} async-done(((bf16[16,128,256]{2,1,0:T(8,128)(2,1)}), bf16[16,128,256]{2,1,0:T(8,128)(2,1)S(1)}, u32[]{:S(2)}, u32[]{:S(2)}) %all-to-all-start.2) | async-done | bytes 1048608 | tf_op jit(solution)/shard_map/all_to_all | solution.py:179
  100.8 0.0 copy-done
  100.8 0.0 copy-done.1
  100.8 0.0 copy-start.3
  100.8 1.2 copy-done.3
  102.0 0.0 copy-start.5
  102.0 1.2 copy-done.5
  103.2 0.0 copy-start.7
  103.2 1.2 copy-done.7
  104.5 0.0 copy-start.9
  104.5 1.2 copy-done.9
  105.7 4.9 %shard_map.88 = (bf16[128,256]{1,0:T(8,128)(2,1)S(1)}, bf16[2,512,512]{2,1,0:T(8,128)(2,1)}, bf16[2,512,512]{2,1,0:T(8,128)(2,1)}) custom-call(s32[2]{0:T(128)S(1)} %pad_add_fusion.where, bf16[16,128,256]{2,1,0:T(8,128)(2,1)S(1)} %all-to-all-done.2.gathered, bf16[2,512,512]{2,1,0:T(8,128)(2,1)S(1)} %copy-done.3, bf16[2,512,512]{2,1,0:T(8,128)(2,1)S(1)} %copy-done.5, ...), custom_call_target="tpu_custom_call" | custom-call | tf_op jit(solution)/shard_map/pallas_call | solution.py:152
  110.7 30.7 %all_to_all.26 = bf16[64,2,256]{2,1,0:T(2,128)(2,1)S(1)} all-to-all(bf16[64,2,256]{2,1,0:T(2,128)(2,1)S(1)} %reshape.24), channel_id=1, replica_groups=mesh['replica'=16,'owner'=64] {'owner'}, dimensions={0} | all-to-all | bytes 131072 | tf_op jit(solution)/shard_map/all_to_all | solution.py:189
  141.4 0.2 shard_map.89
  141.6 16.3 %all_to_all.27.pieces = bf16[16,192,128]{2,1,0:T(8,128)(2,1)S(1)} all-to-all(bf16[16,192,128]{2,1,0:T(8,128)(2,1)S(1)} %shard_map.89), channel_id=1, replica_groups=mesh['replica'=16,'owner'=64] {'replica'}, dimensions={0} | all-to-all | bytes 1572864 | tf_op jit(solution)/shard_map/all_to_all | solution.py:195
  157.9 1.2 shard_map.90
  (4 shorter events, 0.1 us)
Async XLA Ops:
  0.6 18.9 %copy-start.13 = (s32[96]{0:T(128)S(1)}, s32[96]{0:T(128)}, u32[]{:S(2)}) copy-start(s32[96]{0:T(128)} %param.7) | copy-start | bytes 1156
  0.6 1.1 copy-start.10
  3.0 26.7 %all-to-all-start = ((bf16[16,192,128]{2,1,0:T(8,128)(2,1)}), bf16[16,192,128]{2,1,0:T(8,128)(2,1)S(1)}, u32[]{:S(2)}, u32[]{:S(2)}) async-start(bf16[16,192,128]{2,1,0:T(8,128)(2,1)} %shard_map.85), calls=%async_computation | async-start | bytes 1572864 | tf_op jit(solution)/shard_map/all_to_all | solution.py:169
  19.8 1.6 %copy-start.11 = (f32[2,512,512]{2,1,0:T(8,128)S(1)}, f32[2,512,512]{2,1,0:T(8,128)}, u32[]{:S(2)}) copy-start(f32[2,512,512]{2,1,0:T(8,128)} %left.1) | copy-start | bytes 6291460
  21.4 1.6 copy-start.12
  24.0 1.0 copy-start.2
  24.9 1.0 copy-start.4
  25.9 1.0 copy-start.6
  26.9 1.0 copy-start.8
  29.7 71.0 %copy-start = (bf16[2,512,512]{2,1,0:T(8,128)(2,1)S(1)}, bf16[2,512,512]{2,1,0:T(8,128)(2,1)}, u32[]{:S(2)}) copy-start(bf16[2,512,512]{2,1,0:T(8,128)(2,1)} %first_old.1) | copy-start | bytes 3145732
  29.7 71.0 %copy-start.1 = (bf16[2,512,512]{2,1,0:T(8,128)(2,1)S(1)}, bf16[2,512,512]{2,1,0:T(8,128)(2,1)}, u32[]{:S(2)}) copy-start(bf16[2,512,512]{2,1,0:T(8,128)(2,1)} %second_old.1) | copy-start | bytes 3145732
  80.5 20.3 %all-to-all-start.2 = ((bf16[16,128,256]{2,1,0:T(8,128)(2,1)}), bf16[16,128,256]{2,1,0:T(8,128)(2,1)S(1)}, u32[]{:S(2)}, u32[]{:S(2)}) async-start(bf16[16,128,256]{2,1,0:T(8,128)(2,1)} %broadcast_in_dim.12), calls=%async_computation.2 | async-start | bytes 2097152 | tf_op jit(solution)/shard_map/all_to_all | solution.py:179
  100.8 1.2 copy-start.3
  102.0 1.2 copy-start.5
  103.2 1.2 copy-start.7
  104.5 1.2 copy-start.9

commit v2 on v1

v2 whole, which is shorter than its diff:
```python
import functools

import jax
import jax.numpy as jnp
from jax import lax
from jax.experimental import pallas as pl
from jax.experimental.pallas import tpu as pltpu
from jax.sharding import PartitionSpec as P

beta_first = 0.9
beta_second = 0.95
bias_first = 1.0 - 0.9**20
bias_second = 1.0 - 0.95**20
epsilon = 1e-08

PAIRS = 4
TILES = 4
PIECES = PAIRS * TILES
LANES = 128
GROUP = 16

f32 = jnp.float32
bf16 = jnp.bfloat16


def dot(a, b):
    return jnp.dot(a, b, preferred_element_type=f32)


def permutation(dtype):
    out = lax.broadcasted_iota(jnp.int32, (8 * GROUP, 8 * GROUP), 0)
    src = lax.broadcasted_iota(jnp.int32, (8 * GROUP, 8 * GROUP), 1)
    pair = out >> 5
    block = (out & 31) >> 1
    return (src == block * 8 + pair * 2 + (out & 1)).astype(dtype)


def inverse_permutation(dtype):
    out = lax.broadcasted_iota(jnp.int32, (8 * GROUP, 8 * GROUP), 0)
    src = lax.broadcasted_iota(jnp.int32, (8 * GROUP, 8 * GROUP), 1)
    pair = src >> 5
    block = (src & 31) >> 1
    return (out == block * 8 + pair * 2 + (src & 1)).astype(dtype)


def cut_kernel(owner, strips, pieces, slots):
    count = owner.shape[1]
    across = jnp.broadcast_to(owner[...], (count, count)).astype(f32)
    earlier = lax.broadcasted_iota(jnp.int32, (count, count), 0) < lax.broadcasted_iota(
        jnp.int32, (count, count), 1
    )
    level = jnp.sum(((across == across.T) & earlier).astype(f32), axis=0, keepdims=True)
    slot = 2.0 * owner[...].astype(f32) + level
    double = lax.broadcasted_iota(jnp.int32, (count, 2 * count), 0) == (
        lax.broadcasted_iota(jnp.int32, (count, 2 * count), 1) >> 1
    )
    slots[...] = dot(slot.astype(bf16), double.astype(bf16))
    perm = permutation(bf16)
    for g in range(strips.shape[0] // (8 * GROUP)):
        moved = dot(perm, strips[g * 128 : (g + 1) * 128, :]).astype(bf16)
        for pair in range(PAIRS):
            for tile in range(TILES):
                pieces[pair * TILES + tile, g * 32 : (g + 1) * 32, :] = moved[
                    pair * 32 : (pair + 1) * 32, tile * LANES : (tile + 1) * LANES
                ]


def join_kernel(pieces, strips):
    perm = inverse_permutation(bf16)
    for g in range(strips.shape[0] // (8 * GROUP)):
        rows = [
            jnp.concatenate(
                [pieces[pair * TILES + tile, g * 32 : (g + 1) * 32, :] for tile in range(TILES)],
                axis=1,
            )
            for pair in range(PAIRS)
        ]
        strips[g * 128 : (g + 1) * 128, :] = dot(perm, jnp.concatenate(rows, axis=0)).astype(bf16)


def onehot(slots, level):
    dims = (128, slots.shape[1])
    out = lax.broadcasted_iota(jnp.int32, dims, 0)
    src = lax.broadcasted_iota(jnp.int32, dims, 1)
    here = slots[...] == (2 * (out >> 1) + level).astype(f32)
    return (here & ((out & 1) == (src & 1))).astype(bf16)


def place_kernel(pieces, slots, placed):
    total = pieces[0].astype(f32)
    for k in range(1, PIECES):
        total = total + pieces[k].astype(f32)
    total = total.astype(bf16)
    for level in range(2):
        lanes = slice(level * LANES, (level + 1) * LANES)
        placed[:, lanes] = dot(onehot(slots, level), total).astype(bf16)


def spread_kernel(moved, copies):
    for k in range(PIECES):
        copies[k, :, :] = moved[...]


def step_kernel(
    gathered, left, right, first_old, second_old, piece, first_new, second_new,
    second_held, first_buf, second_buf, rows, cols, sems, load_sem,
):
    replica = lax.axis_index("replica")
    pair, tile = lax.shift_right_logical(replica, 2), replica & 3
    perm = permutation(bf16)
    load = pltpu.make_async_copy(second_old, second_held, load_sem)
    load.start()
    copies = []
    for level in range(2):
        lanes = slice(level * LANES, (level + 1) * LANES)
        parts = [
            dot(perm, left[level, g * 128 : (g + 1) * 128, :].astype(bf16)) for g in range(PAIRS)
        ]
        turned = []
        for k in range(PAIRS):
            here = jnp.concatenate([part[k * 32 : (k + 1) * 32] for part in parts], axis=0)
            rows[level, k * 128 : (k + 1) * 128, :] = here.astype(bf16)
            turned.append(here.T.astype(bf16))
        left_t = jnp.concatenate(turned, axis=1)
        right_b = right[level].astype(bf16)
        cols[level, :, :] = right[level].T.astype(bf16)
        grad = jnp.concatenate(
            [
                jnp.concatenate(
                    [gathered[pair * TILES + tile, :, lanes] for tile in range(TILES)], axis=1
                )
                for pair in range(PAIRS)
            ],
            axis=0,
        )
        half = dot(left_t, grad).astype(bf16)
        rotated = dot(half, right_b)
        if level == 0:
            load.wait()
        first = beta_first * first_old[level].astype(f32) + (1.0 - beta_first) * rotated
        second = (
            beta_second * second_held[level].astype(f32) + (1.0 - beta_second) * rotated * rotated
        )
        first_buf[level, :, :] = first.astype(bf16)
        second_buf[level, :, :] = second.astype(bf16)
        for k, (buf, new) in enumerate([(first_buf, first_new), (second_buf, second_new)]):
            copy = pltpu.make_async_copy(buf.at[level], new.at[level], sems.at[level, k])
            copy.start()
            copies.append(copy)
        update = ((first / bias_first) / (jnp.sqrt(second / bias_second) + epsilon)).astype(bf16)
        mine = rows[level, pl.ds(pl.multiple_of(pair * 128, 128), 128), :]
        left_half = dot(mine, update).astype(bf16)
        back = cols[level, :, pl.ds(pl.multiple_of(tile * LANES, LANES), LANES)]
        piece[:, lanes] = dot(left_half, back).astype(bf16)
    for copy in copies:
        copy.wait()


def pick_kernel(returned, slots, copies):
    mine = sum(
        lax.dot_general(
            onehot(slots, level),
            returned[:, level * LANES : (level + 1) * LANES],
            (((0,), (0,)), ((), ())),
            preferred_element_type=f32,
        )
        for level in range(2)
    ).astype(bf16)
    for k in range(PIECES):
        copies[k, :, :] = mine


VMEM = pl.BlockSpec(memory_space=pltpu.VMEM)
ANY = pl.BlockSpec(memory_space=pl.ANY)


def shape(dims, dtype):
    return jax.ShapeDtypeStruct(dims, dtype)


def call(kernel, out, inputs, specs=None, outs=None, scratch=(), limit=8, cost=None):
    single = not isinstance(out, (list, tuple))
    return pl.pallas_call(
        kernel,
        out_shape=out,
        in_specs=specs or [VMEM] * len(inputs),
        out_specs=outs or (VMEM if single else [VMEM] * len(out)),
        scratch_shapes=scratch,
        cost_estimate=cost,
        compiler_params=pltpu.CompilerParams(vmem_limit_bytes=limit * 2**20),
    )(*inputs)


def local(grad_parts, block_owner, left_basis, right_basis, first_moment, second_moment):
    count, rows, width = grad_parts.shape[1:]
    strips = grad_parts.reshape(count * rows, width)
    slot_row = shape((1, 2 * count), f32)
    pieces, slots = call(
        cut_kernel,
        [shape((PIECES, count * 2, LANES), bf16), slot_row],
        (block_owner[None, :], strips),
    )
    parts = lax.all_to_all(pieces, "replica", 0, 0)
    wide = shape((2, width, width), bf16)
    placed = call(place_kernel, shape((128, 2 * LANES), bf16), (parts, slots))
    moved = lax.all_to_all(placed.reshape(64, 2, 2 * LANES), "owner", 0, 0).reshape(128, 2 * LANES)
    copies = call(spread_kernel, shape((PIECES, 128, 2 * LANES), bf16), (moved,))
    gathered = lax.all_to_all(copies, "replica", 0, 0)
    piece, first, second = call(
        step_kernel,
        [shape((128, 2 * LANES), bf16), wide, wide],
        (gathered, left_basis, right_basis, first_moment, second_moment),
        specs=[VMEM] * 4 + [ANY],
        outs=[VMEM, ANY, ANY],
        scratch=[pltpu.VMEM((2, width, width), bf16)] * 5
        + [
            pltpu.SemaphoreType.DMA((2, 2)),
            pltpu.SemaphoreType.DMA,
        ],
        limit=16,
    )
    returned = lax.all_to_all(piece.reshape(64, 2, 2 * LANES), "owner", 0, 0)
    copies = call(
        pick_kernel,
        shape((PIECES, count * 2, LANES), bf16),
        (returned.reshape(128, 2 * LANES), slots),
    )
    joined = lax.all_to_all(copies, "replica", 0, 0)
    direction = call(join_kernel, shape((count * rows, width), bf16), (joined,))
    return direction.reshape(count, rows, width), first, second


def solution(mesh):
    return jax.shard_map(
        local,
        mesh=mesh,
        in_specs=(
            P("replica", None, "owner", None),
            P(),
            P("owner", None, None),
            P("owner", None, None),
            P("owner", None, None),
            P("owner", None, None),
        ),
        out_specs=(P(None, "owner", None), P("owner", None, None), P("owner", None, None)),
        check_vma=False,
    )
```

time: 160 us -> 154 us (0.963)
  blocking collectives: 96.3 us -> 142 us
  starting transfers between devices: 21.4 us -> 0 us
  waiting for transfers between devices: 17.2 us -> 0 us
  local copies, waits for them, and re-layouts: 14.6 us -> 3.15 us
  Pallas kernels: 8.85 us -> 7.23 us
    all_to_all x0 -> x2, blocking collectives: none -> 45.5 us  [the longest x1 25.5 us: local(): parts = lax.all_to_all(pieces, 'replica', 0, 0)]
    all_to_all x2 -> x0, starting transfers between devices: 21.4 us -> none  [the longest x1 16.5 us: local(): parts = lax.all_to_all(pieces, 'replica', 0, 0)]
    all_to_all x2 -> x0, waiting for transfers between devices: 17.2 us -> none  [the longest x1 15.3 us: local(): lax.all_to_all(jnp.broadcast_to(moved[None], (PIECES, 128, 2 * LANES)), '...]
    unnamed x28 -> x12, local copies, waits for them, and re-layouts: 13.1 us -> 3.02 us
    pallas_call x6, Pallas kernels: 8.85 us -> 7.23 us  [call(): pl.pallas_call(kernel, out_shape=out, in_specs=specs or [VMEM] * len(inpu...]
  transfers between devices with their start and end apart: 2 -> 0, of which waited for: 2 -> 0; matrix products, arithmetic and copies ran while one was open for 0% -> 0% of each run, Pallas kernels for 1% -> 0%
where the time goes in v2:
time: 154 us; the launch traced here: 153 us
  blocking collectives  142 us (92%)
  Pallas kernels  7.23 us (5%)
  local copies, waits for them, and re-layouts  3.15 us (2%)
    all_to_all x1, blocking collectives, local(): lax.all_to_all(placed.reshape(64, 2, 2 * LANES), 'owner', 0, 0)  50 us
    all_to_all x1, blocking collectives, local(): returned = lax.all_to_all(piece.reshape(64, 2, 2 * LANES), 'owner', 0, 0)  30.2 us
    all_to_all x1, blocking collectives, local(): parts = lax.all_to_all(pieces, 'replica', 0, 0)  25.5 us
    all_to_all x1, blocking collectives, local(): gathered = lax.all_to_all(copies, 'replica', 0, 0)  19.9 us
    all_to_all x1, blocking collectives, local(): joined = lax.all_to_all(copies, 'replica', 0, 0)  16.3 us
    pallas_call x6, Pallas kernels, call(): pl.pallas_call(kernel, out_shape=out, in_specs=specs or [VMEM] * len(inpu...  7.23 us

profile of v2, /device:TPU:8, one launch (start us, length us, event | category | flops | bytes accessed | tf_op | source)
XLA Modules:
  0.0 153.2 jit_solution(2103915907830780457)
XLA Ops:
  0.6 0.0 copy-start.4
  0.6 1.1 copy-done.4
  1.8 0.0 copy-start.5
  1.8 0.7 copy-done.5
  2.4 0.4 shard_map.85
  2.9 0.0 copy-start.2
  2.9 25.5 %all_to_all.25.pieces = bf16[16,192,128]{2,1,0:T(8,128)(2,1)S(1)} all-to-all(bf16[16,192,128]{2,1,0:T(8,128)(2,1)S(1)} %get-tuple-element.8), channel_id=1, replica_groups=mesh['replica'=16,'owner'=64] {'replica'}, dimensions={0} | all-to-all | bytes 1572864 | tf_op jit(solution)/shard_map/all_to_all | solution.py:203
  28.4 0.0 copy-start
  28.4 0.3 shard_map.86
  28.7 50.0 %all_to_all.26 = bf16[64,2,256]{2,1,0:T(2,128)(2,1)S(1)} all-to-all(bf16[64,2,256]{2,1,0:T(2,128)(2,1)S(1)} %reshape.25), channel_id=1, replica_groups=mesh['replica'=16,'owner'=64] {'owner'}, dimensions={0} | all-to-all | bytes 131072 | tf_op jit(solution)/shard_map/all_to_all | solution.py:206
  78.8 0.0 copy-start.1
  78.8 0.1 shard_map.87
  78.9 19.9 %all_to_all.27.gathered = bf16[16,128,256]{2,1,0:T(8,128)(2,1)S(1)} all-to-all(bf16[16,128,256]{2,1,0:T(8,128)(2,1)S(1)} %shard_map.87), channel_id=1, replica_groups=mesh['replica'=16,'owner'=64] {'replica'}, dimensions={0} | all-to-all | bytes 2097152 | tf_op jit(solution)/shard_map/all_to_all | solution.py:208
  98.8 0.0 copy-done.2
  98.8 0.0 copy-done
  98.8 0.0 copy-done.1
  98.8 0.0 copy-start.3
  98.8 1.2 copy-done.3
  100.1 5.0 %shard_map.88 = (bf16[128,256]{1,0:T(8,128)(2,1)S(1)}, bf16[2,512,512]{2,1,0:T(8,128)(2,1)}, bf16[2,512,512]{2,1,0:T(8,128)(2,1)}) custom-call(bf16[16,128,256]{2,1,0:T(8,128)(2,1)S(1)} %all_to_all.27.gathered, f32[2,512,512]{2,1,0:T(8,128)S(1)} %copy-done, f32[2,512,512]{2,1,0:T(8,128)S(1)} %copy-done.1, bf16[2,512,512]{2,1,0:T(8,128)(2,1)S(1)} %copy-done.2, ...), custom_call_target="tpu_custom_call" | custom-call | tf_op jit(solution)/shard_map/pallas_call | solution.py:183
  105.1 30.2 %all_to_all.28 = bf16[64,2,256]{2,1,0:T(2,128)(2,1)S(1)} all-to-all(bf16[64,2,256]{2,1,0:T(2,128)(2,1)S(1)} %reshape.27), channel_id=1, replica_groups=mesh['replica'=16,'owner'=64] {'owner'}, dimensions={0} | all-to-all | bytes 131072 | tf_op jit(solution)/shard_map/all_to_all | solution.py:222
  135.3 0.3 shard_map.89
  135.6 16.3 %all_to_all.29.pieces = bf16[16,192,128]{2,1,0:T(8,128)(2,1)S(1)} all-to-all(bf16[16,192,128]{2,1,0:T(8,128)(2,1)S(1)} %shard_map.89), channel_id=1, replica_groups=mesh['replica'=16,'owner'=64] {'replica'}, dimensions={0} | all-to-all | bytes 1572864 | tf_op jit(solution)/shard_map/all_to_all | solution.py:228
  151.9 1.2 shard_map.90
  (4 shorter events, 0.1 us)
Async XLA Ops:
  0.6 1.1 copy-start.4
  1.8 0.7 copy-start.5
  2.9 96.0 %copy-start.2 = (bf16[2,512,512]{2,1,0:T(8,128)(2,1)S(1)}, bf16[2,512,512]{2,1,0:T(8,128)(2,1)}, u32[]{:S(2)}) copy-start(bf16[2,512,512]{2,1,0:T(8,128)(2,1)} %first_old.1) | copy-start | bytes 3145732
  28.4 70.4 %copy-start = (f32[2,512,512]{2,1,0:T(8,128)S(1)}, f32[2,512,512]{2,1,0:T(8,128)}, u32[]{:S(2)}) copy-start(f32[2,512,512]{2,1,0:T(8,128)} %left.1) | copy-start | bytes 6291460
  78.8 20.0 %copy-start.1 = (f32[2,512,512]{2,1,0:T(8,128)S(1)}, f32[2,512,512]{2,1,0:T(8,128)}, u32[]{:S(2)}) copy-start(f32[2,512,512]{2,1,0:T(8,128)} %right.1) | copy-start | bytes 6291460
  98.8 1.2 copy-start.3

commit v3 on v2

v3 whole, which is shorter than its diff:
```python
import functools

import jax
import jax.numpy as jnp
from jax import lax
from jax.experimental import pallas as pl
from jax.experimental.pallas import tpu as pltpu
from jax.sharding import PartitionSpec as P

beta_first = 0.9
beta_second = 0.95
bias_first = 1.0 - 0.9**20
bias_second = 1.0 - 0.95**20
epsilon = 1e-08

PAIRS = 4
TILES = 4
PIECES = PAIRS * TILES
LANES = 128
GROUP = 16

f32 = jnp.float32
bf16 = jnp.bfloat16


def dot(a, b):
    return jnp.dot(a, b, preferred_element_type=f32)


def permutation(dtype):
    out = lax.broadcasted_iota(jnp.int32, (8 * GROUP, 8 * GROUP), 0)
    src = lax.broadcasted_iota(jnp.int32, (8 * GROUP, 8 * GROUP), 1)
    pair = out >> 5
    block = (out & 31) >> 1
    return (src == block * 8 + pair * 2 + (out & 1)).astype(dtype)


def inverse_permutation(dtype):
    out = lax.broadcasted_iota(jnp.int32, (8 * GROUP, 8 * GROUP), 0)
    src = lax.broadcasted_iota(jnp.int32, (8 * GROUP, 8 * GROUP), 1)
    pair = src >> 5
    block = (src & 31) >> 1
    return (out == block * 8 + pair * 2 + (src & 1)).astype(dtype)


def cut_kernel(strips_hbm, pieces, strips, sems):
    groups = strips.shape[0] // (8 * GROUP)
    loads = []
    for g in range(groups):
        part = pl.ds(g * 128, 128)
        loads.append(pltpu.make_async_copy(strips_hbm.at[part], strips.at[part], sems.at[g]))
        loads[-1].start()
    perm = permutation(bf16)
    for g in range(groups):
        loads[g].wait()
        moved = dot(perm, strips[g * 128 : (g + 1) * 128, :]).astype(bf16)
        for pair in range(PAIRS):
            for tile in range(TILES):
                pieces[pair * TILES + tile, g * 32 : (g + 1) * 32, :] = moved[
                    pair * 32 : (pair + 1) * 32, tile * LANES : (tile + 1) * LANES
                ]


def join_kernel(pieces, strips_hbm, strips, sems):
    perm = inverse_permutation(bf16)
    stores = []
    for g in range(strips.shape[0] // (8 * GROUP)):
        rows = [
            jnp.concatenate(
                [pieces[pair * TILES + tile, g * 32 : (g + 1) * 32, :] for tile in range(TILES)],
                axis=1,
            )
            for pair in range(PAIRS)
        ]
        part = pl.ds(g * 128, 128)
        strips[g * 128 : (g + 1) * 128, :] = dot(perm, jnp.concatenate(rows, axis=0)).astype(bf16)
        stores.append(pltpu.make_async_copy(strips.at[part], strips_hbm.at[part], sems.at[g]))
        stores[-1].start()
    for store in stores:
        store.wait()


def onehot(slots, level):
    dims = (128, slots.shape[1])
    out = lax.broadcasted_iota(jnp.int32, dims, 0)
    src = lax.broadcasted_iota(jnp.int32, dims, 1)
    here = slots[...] == (2 * (out >> 1) + level).astype(f32)
    return (here & ((out & 1) == (src & 1))).astype(bf16)


def prep_kernel(
    owner, left, right, slots, mine, left_t, right_b, turned, rows, cols, left_buf, right_buf, sems
):
    count = owner.shape[1]
    across = jnp.broadcast_to(owner[...], (count, count)).astype(f32)
    earlier = lax.broadcasted_iota(jnp.int32, (count, count), 0) < lax.broadcasted_iota(
        jnp.int32, (count, count), 1
    )
    level = jnp.sum(((across == across.T) & earlier).astype(f32), axis=0, keepdims=True)
    slot = 2.0 * owner[...].astype(f32) + level
    double = lax.broadcasted_iota(jnp.int32, (count, 2 * count), 0) == (
        lax.broadcasted_iota(jnp.int32, (count, 2 * count), 1) >> 1
    )
    slots[...] = dot(slot.astype(bf16), double.astype(bf16))
    replica = lax.axis_index("replica")
    pair, tile = lax.shift_right_logical(replica, 2), replica & 3
    perm = permutation(bf16)
    copies = []
    for level in range(2):
        parts = [
            dot(perm, left[level, g * 128 : (g + 1) * 128, :].astype(bf16)) for g in range(PAIRS)
        ]
        for k in range(PAIRS):
            here = jnp.concatenate([part[k * 32 : (k + 1) * 32] for part in parts], axis=0)
            rows[level, k * 128 : (k + 1) * 128, :] = here.astype(bf16)
            left_buf[level, :, k * 128 : (k + 1) * 128] = here.T.astype(bf16)
        right_buf[level, :, :] = right[level, :, :].astype(bf16)
        cols[level, :, :] = right[level, :, :].T.astype(bf16)
        part = pl.ds(pl.multiple_of(pair * 128, 128), 128)
        lanes = pl.ds(pl.multiple_of(tile * LANES, LANES), LANES)
        for k, (src, dst) in enumerate(
            [
                (left_buf.at[level], left_t.at[level]),
                (right_buf.at[level], right_b.at[level]),
                (rows.at[level, part], mine.at[level]),
                (cols.at[level, :, lanes], turned.at[level]),
            ]
        ):
            copies.append(pltpu.make_async_copy(src, dst, sems.at[level, k]))
            copies[-1].start()
    for copy in copies:
        copy.wait()


def place_kernel(pieces, slots, placed):
    total = pieces[0].astype(f32)
    for k in range(1, PIECES):
        total = total + pieces[k].astype(f32)
    total = total.astype(bf16)
    for level in range(2):
        lanes = slice(level * LANES, (level + 1) * LANES)
        placed[:, lanes] = dot(onehot(slots, level), total).astype(bf16)


def spread_kernel(moved, copies):
    for k in range(PIECES):
        for level in range(2):
            copies[k, level * 128 : (level + 1) * 128, :] = moved[
                :, level * LANES : (level + 1) * LANES
            ]


def step_kernel(
    gathered, mine, left_t, right_b, turned, first_old, second_old, piece, first_new, second_new,
    first_held, second_held, first_buf, second_buf, sems, load_sems,
):
    loads = []
    for level in range(2):
        for k, (old, held) in enumerate([(first_old, first_held), (second_old, second_held)]):
            load = pltpu.make_async_copy(old.at[level], held.at[level], load_sems.at[level, k])
            load.start()
            loads.append(load)
    copies = []
    for level in range(2):
        grad = jnp.concatenate(
            [
                jnp.concatenate(
                    [
                        gathered[pair * TILES + tile, level * 128 : (level + 1) * 128, :]
                        for tile in range(TILES)
                    ],
                    axis=1,
                )
                for pair in range(PAIRS)
            ],
            axis=0,
        )
        half = dot(left_t[level], grad).astype(bf16)
        rotated = dot(half, right_b[level])
        loads[2 * level].wait()
        loads[2 * level + 1].wait()
        first = beta_first * first_held[level].astype(f32) + (1.0 - beta_first) * rotated
        second = beta_second * second_held[level].astype(f32) + (
            (1.0 - beta_second) * rotated
        ) * rotated
        first_buf[level, :, :] = first.astype(bf16)
        second_buf[level, :, :] = second.astype(bf16)
        for k, (buf, new) in enumerate([(first_buf, first_new), (second_buf, second_new)]):
            copy = pltpu.make_async_copy(buf.at[level], new.at[level], sems.at[level, k])
            copy.start()
            copies.append(copy)
        scaled = second * (1.0 / bias_second)
        update = (first * (1.0 / bias_first)) / (scaled * lax.rsqrt(scaled) + epsilon)
        left_half = dot(mine[level], update.astype(bf16)).astype(bf16)
        lanes = slice(level * LANES, (level + 1) * LANES)
        piece[:, lanes] = dot(left_half, turned[level]).astype(bf16)
    for copy in copies:
        copy.wait()


def pick_kernel(returned, slots, copies):
    mine = sum(
        lax.dot_general(
            onehot(slots, level),
            returned[:, level * LANES : (level + 1) * LANES],
            (((0,), (0,)), ((), ())),
            preferred_element_type=f32,
        )
        for level in range(2)
    ).astype(bf16)
    for k in range(PIECES):
        copies[k, :, :] = mine


VMEM = pl.BlockSpec(memory_space=pltpu.VMEM)
HBM = pl.BlockSpec(memory_space=pltpu.HBM)


def shape(dims, dtype):
    return jax.ShapeDtypeStruct(dims, dtype)


def in_hbm(array):
    return pltpu.with_memory_space_constraint(array, pltpu.HBM)


def call(kernel, out, inputs, specs=None, outs=None, scratch=(), limit=8, cost=None):
    single = not isinstance(out, (list, tuple))
    return pl.pallas_call(
        kernel,
        out_shape=out,
        in_specs=specs or [VMEM] * len(inputs),
        out_specs=outs or (VMEM if single else [VMEM] * len(out)),
        scratch_shapes=scratch,
        cost_estimate=cost,
        compiler_params=pltpu.CompilerParams(vmem_limit_bytes=limit * 2**20),
    )(*inputs)


def local(grad_parts, block_owner, left_basis, right_basis, first_moment, second_moment):
    count, rows, width = grad_parts.shape[1:]
    strips = grad_parts.reshape(count * rows, width)
    slot_row = shape((1, 2 * count), f32)
    groups = count // GROUP
    pieces = call(
        cut_kernel,
        shape((PIECES, count * 2, LANES), bf16),
        (in_hbm(strips),),
        specs=[HBM],
        scratch=[
            pltpu.VMEM((count * rows, width), bf16),
            pltpu.SemaphoreType.DMA((groups,)),
        ],
    )
    parts = lax.all_to_all(pieces, "replica", 0, 0)
    wide_hbm = pltpu.HBM((2, width, width), bf16)
    held = pltpu.VMEM((2, width, width), bf16)
    slots, mine, left_t, right_b, turned = call(
        prep_kernel,
        [
            slot_row,
            pltpu.HBM((2, 128, width), bf16),
            wide_hbm,
            wide_hbm,
            pltpu.HBM((2, width, LANES), bf16),
        ],
        (block_owner[None, :], left_basis, right_basis),
        outs=[VMEM] + [HBM] * 4,
        scratch=[held] * 4 + [pltpu.SemaphoreType.DMA((2, 4))],
        limit=16,
        cost=pl.CostEstimate(flops=4 * 10**9, bytes_accessed=8 * 2**20, transcendentals=0),
    )
    placed = call(place_kernel, shape((128, 2 * LANES), bf16), (parts, slots))
    moved = lax.all_to_all(placed.reshape(64, 2, 2 * LANES), "owner", 0, 0).reshape(128, 2 * LANES)
    copies = call(spread_kernel, shape((PIECES, 2 * 128, LANES), bf16), (moved,))
    gathered = lax.all_to_all(copies, "replica", 0, 0)
    piece, first, second = call(
        step_kernel,
        [shape((128, 2 * LANES), bf16), wide_hbm, wide_hbm],
        (gathered, mine, left_t, right_b, turned, in_hbm(first_moment), in_hbm(second_moment)),
        specs=[VMEM] * 5 + [HBM] * 2,
        outs=[VMEM, HBM, HBM],
        scratch=[held] * 4 + [pltpu.SemaphoreType.DMA((2, 2))] * 2,
        limit=16,
    )
    returned = lax.all_to_all(piece.reshape(64, 2, 2 * LANES), "owner", 0, 0)
    copies = call(
        pick_kernel,
        shape((PIECES, count * 2, LANES), bf16),
        (returned.reshape(128, 2 * LANES), slots),
    )
    joined = lax.all_to_all(copies, "replica", 0, 0)
    direction = call(
        join_kernel,
        pltpu.HBM((count * rows, width), bf16),
        (joined,),
        outs=HBM,
        scratch=[
            pltpu.VMEM((count * rows, width), bf16),
            pltpu.SemaphoreType.DMA((groups,)),
        ],
    )
    return direction.reshape(count, rows, width), first, second


def solution(mesh):
    return jax.shard_map(
        local,
        mesh=mesh,
        in_specs=(
            P("replica", None, "owner", None),
            P(),
            P("owner", None, None),
            P("owner", None, None),
            P("owner", None, None),
            P("owner", None, None),
        ),
        out_specs=(P(None, "owner", None), P("owner", None, None), P("owner", None, None)),
        check_vma=False,
    )
```

time: 154 us -> 152 us (0.987)
  blocking collectives: 142 us -> 115 us
  starting transfers between devices: 0 us -> 16.5 us
  waiting for transfers between devices: 0 us -> 6.48 us
  Pallas kernels: 7.23 us -> 11.2 us
    all_to_all x1 -> x0, blocking collectives: 25.5 us -> none  [local(): parts = lax.all_to_all(pieces, 'replica', 0, 0)]
    all_to_all x0 -> x1, starting transfers between devices: none -> 16.5 us  [local(): parts = lax.all_to_all(pieces, 'replica', 0, 0)]
    all_to_all x0 -> x1, waiting for transfers between devices: none -> 6.48 us  [local(): parts = lax.all_to_all(pieces, 'replica', 0, 0)]
    pallas_call x6 -> x7, Pallas kernels: 7.23 us -> 11.2 us  [call(): pl.pallas_call(kernel, out_shape=out, in_specs=specs or [VMEM] * len(inpu...]
  transfers between devices with their start and end apart: 0 -> 1, of which waited for: 0 -> 1; matrix products, arithmetic and copies ran while one was open for 0% -> 0% of each run, Pallas kernels for 0% -> 1%
where the time goes in v3:
time: 152 us
  blocking collectives  115 us (76%)
  starting transfers between devices  16.5 us (11%)
  Pallas kernels  11.2 us (7%)
  waiting for transfers between devices  6.48 us (4%)
  local copies, waits for them, and re-layouts  1.75 us (1%)
    all_to_all x1, blocking collectives, local(): lax.all_to_all(placed.reshape(64, 2, 2 * LANES), 'owner', 0, 0)  49.3 us
    all_to_all x1, blocking collectives, local(): returned = lax.all_to_all(piece.reshape(64, 2, 2 * LANES), 'owner', 0, 0)  30.2 us
    all_to_all x1, blocking collectives, local(): gathered = lax.all_to_all(copies, 'replica', 0, 0)  19.4 us
    all_to_all x1, starting transfers between devices, local(): parts = lax.all_to_all(pieces, 'replica', 0, 0)  16.5 us
    all_to_all x1, blocking collectives, local(): joined = lax.all_to_all(copies, 'replica', 0, 0)  16.3 us
    pallas_call x7, Pallas kernels, call(): pl.pallas_call(kernel, out_shape=out, in_specs=specs or [VMEM] * len(inpu...  11.2 us
    all_to_all x1, waiting for transfers between devices, local(): parts = lax.all_to_all(pieces, 'replica', 0, 0)  6.48 us
  transfers between devices with their start and end apart: 1, of which 1 were waited for; matrix products, arithmetic and copies ran while one was open for 0% of the time, Pallas kernels for 1%

profile of v3, /device:TPU:8, one launch (start us, length us, event | category | flops | bytes accessed | tf_op | source)
XLA Modules:
  0.0 152.0 jit_solution(8729447969187805964)
XLA Ops:
  0.6 0.0 copy-start.4
  0.6 0.0 copy-start.6
  0.7 3.0 %shard_map.85 = bf16[16,192,128]{2,1,0:T(8,128)(2,1)} custom-call(bf16[768,512]{1,0:T(8,128)(2,1)} %bitcast.4), custom_call_target="tpu_custom_call" | custom-call | tf_op jit(solution)/shard_map/pallas_call | solution.py:229
  3.7 16.5 %all-to-all-start = ((bf16[16,192,128]{2,1,0:T(8,128)(2,1)}), bf16[16,192,128]{2,1,0:T(8,128)(2,1)S(1)}, u32[]{:S(2)}, u32[]{:S(2)}) async-start(bf16[16,192,128]{2,1,0:T(8,128)(2,1)} %shard_map.85), calls=%async_computation | async-start | bytes 1572864 | tf_op jit(solution)/shard_map/all_to_all | solution.py:255
  20.2 0.0 copy-done.4
  20.2 0.0 copy-done.6
  20.2 0.0 copy-start.5
  20.2 1.6 %copy-done.5 = f32[2,512,512]{2,1,0:T(8,128)S(1)} copy-done((f32[2,512,512]{2,1,0:T(8,128)S(1)}, f32[2,512,512]{2,1,0:T(8,128)}, u32[]{:S(2)}) %copy-start.5) | copy-done | bytes 2097176
  21.8 2.1 %shard_map.86 = (f32[1,192]{1,0:T(1,128)S(1)}, bf16[2,128,512]{2,1,0:T(8,128)(2,1)}, bf16[2,512,512]{2,1,0:T(8,128)(2,1)}, bf16[2,512,512]{2,1,0:T(8,128)(2,1)}, bf16[2,512,128]{2,1,0:T(8,128)(2,1)}) custom-call(s32[1,96]{1,0:T(1,128)S(1)} %bitcast.3, f32[2,512,512]{2,1,0:T(8,128)S(1)} %copy-done.4, f32[2,512,512]{2,1,0:T(8,128)S(1)} %copy-done.5), custom_call_target="tpu_custom_call" | custom-call | flops 4000000000 | bytes 8388608 | tf_op jit(solution)/shard_map/pallas_call | solution.py:229
  24.0 6.5 %all-to-all-done.pieces = bf16[16,192,128]{2,1,0:T(8,128)(2,1)S(1)} async-done(((bf16[16,192,128]{2,1,0:T(8,128)(2,1)}), bf16[16,192,128]{2,1,0:T(8,128)(2,1)S(1)}, u32[]{:S(2)}, u32[]{:S(2)}) %all-to-all-start) | async-done | bytes 786464 | tf_op jit(solution)/shard_map/all_to_all | solution.py:255
  30.4 0.0 copy-start
  30.4 0.0 copy-start.1
  30.4 0.0 copy-start.2
  30.4 0.0 copy-start.3
  30.4 0.3 shard_map.87
  30.8 49.3 %all_to_all.25 = bf16[64,2,256]{2,1,0:T(2,128)(2,1)S(1)} all-to-all(bf16[64,2,256]{2,1,0:T(2,128)(2,1)S(1)} %reshape.25), channel_id=1, replica_groups=mesh['replica'=16,'owner'=64] {'owner'}, dimensions={0} | all-to-all | bytes 131072 | tf_op jit(solution)/shard_map/all_to_all | solution.py:274
  80.1 0.1 shard_map.88
  80.3 19.4 %all_to_all.26.gathered = bf16[16,256,128]{2,1,0:T(8,128)(2,1)S(1)} all-to-all(bf16[16,256,128]{2,1,0:T(8,128)(2,1)S(1)} %shard_map.88), channel_id=1, replica_groups=mesh['replica'=16,'owner'=64] {'replica'}, dimensions={0} | all-to-all | bytes 2097152 | tf_op jit(solution)/shard_map/all_to_all | solution.py:276
  99.6 0.0 copy-done
  99.7 0.0 copy-done.1
  99.7 0.0 copy-done.2
  99.7 0.0 copy-done.3
  99.7 4.3 %shard_map.89 = (bf16[128,256]{1,0:T(8,128)(2,1)S(1)}, bf16[2,512,512]{2,1,0:T(8,128)(2,1)}, bf16[2,512,512]{2,1,0:T(8,128)(2,1)}) custom-call(bf16[16,256,128]{2,1,0:T(8,128)(2,1)S(1)} %all_to_all.26.gathered, bf16[2,128,512]{2,1,0:T(8,128)(2,1)S(1)} %copy-done.2, bf16[2,512,512]{2,1,0:T(8,128)(2,1)S(1)} %copy-done, bf16[2,512,512]{2,1,0:T(8,128)(2,1)S(1)} %copy-done.1, ...), custom_call_target="tpu_custom_call" | custom-call | tf_op jit(solution)/shard_map/pallas_call | solution.py:229
  104.0 30.2 %all_to_all.27 = bf16[64,2,256]{2,1,0:T(2,128)(2,1)S(1)} all-to-all(bf16[64,2,256]{2,1,0:T(2,128)(2,1)S(1)} %reshape.27), channel_id=1, replica_groups=mesh['replica'=16,'owner'=64] {'owner'}, dimensions={0} | all-to-all | bytes 131072 | tf_op jit(solution)/shard_map/all_to_all | solution.py:286
  134.3 0.3 shard_map.90
  134.6 16.3 %all_to_all.28.pieces = bf16[16,192,128]{2,1,0:T(8,128)(2,1)S(1)} all-to-all(bf16[16,192,128]{2,1,0:T(8,128)(2,1)S(1)} %shard_map.90), channel_id=1, replica_groups=mesh['replica'=16,'owner'=64] {'replica'}, dimensions={0} | all-to-all | bytes 1572864 | tf_op jit(solution)/shard_map/all_to_all | solution.py:292
  150.9 1.1 shard_map.91
  (4 shorter events, 0.1 us)
Async XLA Ops:
  0.6 19.6 %copy-start.4 = (f32[2,512,512]{2,1,0:T(8,128)S(1)}, f32[2,512,512]{2,1,0:T(8,128)}, u32[]{:S(2)}) copy-start(f32[2,512,512]{2,1,0:T(8,128)} %left.1) | copy-start | bytes 6291460
  0.6 19.6 %copy-start.6 = (s32[96]{0:T(128)S(1)}, s32[96]{0:T(128)}, u32[]{:S(2)}) copy-start(s32[96]{0:T(128)} %param.7) | copy-start | bytes 1156
  3.7 26.7 %all-to-all-start = ((bf16[16,192,128]{2,1,0:T(8,128)(2,1)}), bf16[16,192,128]{2,1,0:T(8,128)(2,1)S(1)}, u32[]{:S(2)}, u32[]{:S(2)}) async-start(bf16[16,192,128]{2,1,0:T(8,128)(2,1)} %shard_map.85), calls=%async_computation | async-start | bytes 1572864 | tf_op jit(solution)/shard_map/all_to_all | solution.py:255
  20.2 1.6 %copy-start.5 = (f32[2,512,512]{2,1,0:T(8,128)S(1)}, f32[2,512,512]{2,1,0:T(8,128)}, u32[]{:S(2)}) copy-start(f32[2,512,512]{2,1,0:T(8,128)} %right.1) | copy-start | bytes 6291460
  30.4 69.2 %copy-start = (bf16[2,512,512]{2,1,0:T(8,128)(2,1)S(1)}, bf16[2,512,512]{2,1,0:T(8,128)(2,1)}, u32[]{:S(2)}) copy-start(bf16[2,512,512]{2,1,0:T(8,128)(2,1)} %get-tuple-element.13.left_t) | copy-start | bytes 3145732
  30.4 69.2 %copy-start.1 = (bf16[2,512,512]{2,1,0:T(8,128)(2,1)S(1)}, bf16[2,512,512]{2,1,0:T(8,128)(2,1)}, u32[]{:S(2)}) copy-start(bf16[2,512,512]{2,1,0:T(8,128)(2,1)} %get-tuple-element.14.right_b) | copy-start | bytes 3145732
  30.4 69.2 %copy-start.2 = (bf16[2,128,512]{2,1,0:T(8,128)(2,1)S(1)}, bf16[2,128,512]{2,1,0:T(8,128)(2,1)}, u32[]{:S(2)}) copy-start(bf16[2,128,512]{2,1,0:T(8,128)(2,1)} %get-tuple-element.12.mine) | copy-start | bytes 786436
  30.4 69.2 %copy-start.3 = (bf16[2,512,128]{2,1,0:T(8,128)(2,1)S(1)}, bf16[2,512,128]{2,1,0:T(8,128)(2,1)}, u32[]{:S(2)}) copy-start(bf16[2,512,128]{2,1,0:T(8,128)(2,1)} %get-tuple-element.15.turned) | copy-start | bytes 786436

commit v4 on v2

--- a/solution.py
+++ b/solution.py
@@ -43,7 +43,12 @@
     return (out == block * 8 + pair * 2 + (src & 1)).astype(dtype)
 
 
-def cut_kernel(owner, strips, pieces, slots):
+def cut_kernel(owner_hbm, strips_hbm, pieces, slots, owner, strips, sems):
+    take = pltpu.make_async_copy(owner_hbm, owner, sems.at[0])
+    take.start()
+    load = pltpu.make_async_copy(strips_hbm, strips, sems.at[1])
+    load.start()
+    take.wait()
     count = owner.shape[1]
     across = jnp.broadcast_to(owner[...], (count, count)).astype(f32)
     earlier = lax.broadcasted_iota(jnp.int32, (count, count), 0) < lax.broadcasted_iota(
@@ -56,6 +61,7 @@
     )
     slots[...] = dot(slot.astype(bf16), double.astype(bf16))
     perm = permutation(bf16)
+    load.wait()
     for g in range(strips.shape[0] // (8 * GROUP)):
         moved = dot(perm, strips[g * 128 : (g + 1) * 128, :]).astype(bf16)
         for pair in range(PAIRS):
@@ -65,7 +71,15 @@
                 ]
 
 
-def join_kernel(pieces, strips):
+def join_kernel(
+    pieces, last_new, first_in, second_in, strips_hbm, first_hbm, second_hbm, strips, sems, out_sems
+):
+    stores = [
+        pltpu.make_async_copy(last_new.at[0], first_hbm.at[1], out_sems.at[0]),
+        pltpu.make_async_copy(last_new.at[1], second_hbm.at[1], out_sems.at[1]),
+    ]
+    for store in stores:
+        store.start()
     perm = inverse_permutation(bf16)
     for g in range(strips.shape[0] // (8 * GROUP)):
         rows = [
@@ -75,7 +89,12 @@
             )
             for pair in range(PAIRS)
         ]
+        part = pl.ds(g * 128, 128)
         strips[g * 128 : (g + 1) * 128, :] = dot(perm, jnp.concatenate(rows, axis=0)).astype(bf16)
+        stores.append(pltpu.make_async_copy(strips.at[part], strips_hbm.at[part], sems.at[g]))
+        stores[-1].start()
+    for store in stores:
+        store.wait()
 
 
 def onehot(slots, level):
@@ -98,21 +117,25 @@
 
 def spread_kernel(moved, copies):
     for k in range(PIECES):
-        copies[k, :, :] = moved[...]
+        for level in range(2):
+            copies[k, level * 128 : (level + 1) * 128, :] = moved[
+                :, level * LANES : (level + 1) * LANES
+            ]
 
 
 def step_kernel(
-    gathered, left, right, first_old, second_old, piece, first_new, second_new,
-    second_held, first_buf, second_buf, rows, cols, sems, load_sem,
+    gathered, left, right, first_old, second_old, piece, first_new, second_new, last_new,
+    first_held, second_held, new, rows, sems, out_sems,
 ):
+    loads = []
+    for level in range(2):
+        for k, (old, held) in enumerate([(first_old, first_held), (second_old, second_held)]):
+            loads.append(pltpu.make_async_copy(old.at[level], held.at[level], sems.at[level, k]))
+            loads[-1].start()
     replica = lax.axis_index("replica")
     pair, tile = lax.shift_right_logical(replica, 2), replica & 3
     perm = permutation(bf16)
-    load = pltpu.make_async_copy(second_old, second_held, load_sem)
-    load.start()
-    copies = []
     for level in range(2):
-        lanes = slice(level * LANES, (level + 1) * LANES)
         parts = [
             dot(perm, left[level, g * 128 : (g + 1) * 128, :].astype(bf16)) for g in range(PAIRS)
         ]
@@ -123,37 +146,46 @@
             turned.append(here.T.astype(bf16))
         left_t = jnp.concatenate(turned, axis=1)
         right_b = right[level].astype(bf16)
-        cols[level, :, :] = right[level].T.astype(bf16)
         grad = jnp.concatenate(
             [
                 jnp.concatenate(
-                    [gathered[pair * TILES + tile, :, lanes] for tile in range(TILES)], axis=1
+                    [
+                        gathered[k * TILES + t, level * 128 : (level + 1) * 128, :]
+                        for t in range(TILES)
+                    ],
+                    axis=1,
                 )
-                for pair in range(PAIRS)
+                for k in range(PAIRS)
             ],
             axis=0,
         )
-        half = dot(left_t, grad).astype(bf16)
-        rotated = dot(half, right_b)
+        rotated = dot(dot(left_t, grad).astype(bf16), right_b)
+        loads[2 * level].wait()
+        loads[2 * level + 1].wait()
+        first = beta_first * first_held[level].astype(f32) + (1.0 - beta_first) * rotated
+        second = beta_second * second_held[level].astype(f32) + (
+            (1.0 - beta_second) * rotated
+        ) * rotated
+        held = last_new if level else new
+        held[0, :, :] = first.astype(bf16)
+        held[1, :, :] = second.astype(bf16)
         if level == 0:
-            load.wait()
-        first = beta_first * first_old[level].astype(f32) + (1.0 - beta_first) * rotated
-        second = (
-            beta_second * second_held[level].astype(f32) + (1.0 - beta_second) * rotated * rotated
-        )
-        first_buf[level, :, :] = first.astype(bf16)
-        second_buf[level, :, :] = second.astype(bf16)
-        for k, (buf, new) in enumerate([(first_buf, first_new), (second_buf, second_new)]):
-            copy = pltpu.make_async_copy(buf.at[level], new.at[level], sems.at[level, k])
-            copy.start()
-            copies.append(copy)
-        update = ((first / bias_first) / (jnp.sqrt(second / bias_second) + epsilon)).astype(bf16)
+            stores = [
+                pltpu.make_async_copy(new.at[k], out.at[0], out_sems.at[k])
+                for k, out in enumerate([first_new, second_new])
+            ]
+            for store in stores:
+                store.start()
+        scaled = second * (1.0 / bias_second)
+        update = (first * (1.0 / bias_first)) / (scaled * lax.rsqrt(scaled) + epsilon)
         mine = rows[level, pl.ds(pl.multiple_of(pair * 128, 128), 128), :]
-        left_half = dot(mine, update).astype(bf16)
-        back = cols[level, :, pl.ds(pl.multiple_of(tile * LANES, LANES), LANES)]
-        piece[:, lanes] = dot(left_half, back).astype(bf16)
-    for copy in copies:
-        copy.wait()
+        left_half = dot(mine, update.astype(bf16)).astype(bf16)
+        back = right[level, pl.ds(pl.multiple_of(tile * LANES, LANES), LANES), :].astype(bf16)
+        piece[:, level * LANES : (level + 1) * LANES] = lax.dot_general(
+            left_half, back, (((1,), (1,)), ((), ())), preferred_element_type=f32
+        ).astype(bf16)
+    for store in stores:
+        store.wait()
 
 
 def pick_kernel(returned, slots, copies):
@@ -171,14 +203,18 @@
 
 
 VMEM = pl.BlockSpec(memory_space=pltpu.VMEM)
-ANY = pl.BlockSpec(memory_space=pl.ANY)
+HBM = pl.BlockSpec(memory_space=pltpu.HBM)
 
 
 def shape(dims, dtype):
     return jax.ShapeDtypeStruct(dims, dtype)
 
 
-def call(kernel, out, inputs, specs=None, outs=None, scratch=(), limit=8, cost=None):
+def in_hbm(array):
+    return pltpu.with_memory_space_constraint(array, pltpu.HBM)
+
+
+def call(kernel, out, inputs, specs=None, outs=None, scratch=(), limit=8, alias=None):
     single = not isinstance(out, (list, tuple))
     return pl.pallas_call(
         kernel,
@@ -186,7 +222,7 @@
         in_specs=specs or [VMEM] * len(inputs),
         out_specs=outs or (VMEM if single else [VMEM] * len(out)),
         scratch_shapes=scratch,
-        cost_estimate=cost,
+        input_output_aliases=alias or {},
         compiler_params=pltpu.CompilerParams(vmem_limit_bytes=limit * 2**20),
     )(*inputs)
 
@@ -195,28 +231,32 @@
     count, rows, width = grad_parts.shape[1:]
     strips = grad_parts.reshape(count * rows, width)
     slot_row = shape((1, 2 * count), f32)
+    groups = count // GROUP
     pieces, slots = call(
         cut_kernel,
         [shape((PIECES, count * 2, LANES), bf16), slot_row],
-        (block_owner[None, :], strips),
+        (in_hbm(block_owner[None, :]), in_hbm(strips)),
+        specs=[HBM, HBM],
+        scratch=[
+            pltpu.VMEM((1, count), jnp.int32),
+            pltpu.VMEM((count * rows, width), bf16),
+            pltpu.SemaphoreType.DMA((2,)),
+        ],
     )
     parts = lax.all_to_all(pieces, "replica", 0, 0)
-    wide = shape((2, width, width), bf16)
+    held = pltpu.VMEM((2, width, width), bf16)
     placed = call(place_kernel, shape((128, 2 * LANES), bf16), (parts, slots))
     moved = lax.all_to_all(placed.reshape(64, 2, 2 * LANES), "owner", 0, 0).reshape(128, 2 * LANES)
-    copies = call(spread_kernel, shape((PIECES, 128, 2 * LANES), bf16), (moved,))
+    copies = call(spread_kernel, shape((PIECES, 2 * 128, LANES), bf16), (moved,))
     gathered = lax.all_to_all(copies, "replica", 0, 0)
-    piece, first, second = call(
+    in_place = pltpu.HBM((2, width, width), bf16)
+    piece, first, second, last_new = call(
         step_kernel,
-        [shape((128, 2 * LANES), bf16), wide, wide],
-        (gathered, left_basis, right_basis, first_moment, second_moment),
-        specs=[VMEM] * 4 + [ANY],
-        outs=[VMEM, ANY, ANY],
-        scratch=[pltpu.VMEM((2, width, width), bf16)] * 5
-        + [
-            pltpu.SemaphoreType.DMA((2, 2)),
-            pltpu.SemaphoreType.DMA,
-        ],
+        [shape((128, 2 * LANES), bf16), in_place, in_place, held],
+        (gathered, left_basis, right_basis, in_hbm(first_moment), in_hbm(second_moment)),
+        specs=[VMEM] * 3 + [HBM] * 2,
+        outs=[VMEM, HBM, HBM, VMEM],
+        scratch=[held] * 4 + [pltpu.SemaphoreType.DMA((2, 2)), pltpu.SemaphoreType.DMA((2,))],
         limit=16,
     )
     returned = lax.all_to_all(piece.reshape(64, 2, 2 * LANES), "owner", 0, 0)
@@ -226,7 +266,23 @@
         (returned.reshape(128, 2 * LANES), slots),
     )
     joined = lax.all_to_all(copies, "replica", 0, 0)
-    direction = call(join_kernel, shape((count * rows, width), bf16), (joined,))
+    direction, first, second = call(
+        join_kernel,
+        [
+            pltpu.HBM((count * rows, width), bf16),
+            in_place,
+            in_place,
+        ],
+        (joined, last_new, in_hbm(first), in_hbm(second)),
+        specs=[VMEM, VMEM, HBM, HBM],
+        outs=[HBM] * 3,
+        alias={2: 1, 3: 2},
+        scratch=[
+            pltpu.VMEM((count * rows, width), bf16),
+            pltpu.SemaphoreType.DMA((groups,)),
+            pltpu.SemaphoreType.DMA((2,)),
+        ],
+    )
     return direction.reshape(count, rows, width), first, second
 
 

time: 154 us -> 151 us (0.981)
  local copies, waits for them, and re-layouts: 3.15 us -> 0.15 us
    unnamed x12 -> x4, local copies, waits for them, and re-layouts: 3.02 us -> 0.01 us
where the time goes in v4:
time: 151 us; the launch traced here: 150 us
  blocking collectives  142 us (94%)
  Pallas kernels  7.42 us (5%)
    all_to_all x1, blocking collectives, local(): lax.all_to_all(placed.reshape(64, 2, 2 * LANES), 'owner', 0, 0)  50 us
    all_to_all x1, blocking collectives, local(): returned = lax.all_to_all(piece.reshape(64, 2, 2 * LANES), 'owner', 0, 0)  30.2 us
    all_to_all x1, blocking collectives, local(): parts = lax.all_to_all(pieces, 'replica', 0, 0)  25.4 us
    all_to_all x1, blocking collectives, local(): gathered = lax.all_to_all(copies, 'replica', 0, 0)  19.9 us
    all_to_all x1, blocking collectives, local(): joined = lax.all_to_all(copies, 'replica', 0, 0)  16.3 us
    pallas_call x6, Pallas kernels, call(): pl.pallas_call(kernel, out_shape=out, in_specs=specs or [VMEM] * len(inpu...  7.42 us

profile of v4, /device:TPU:8, one launch (start us, length us, event | category | flops | bytes accessed | tf_op | source)
XLA Modules:
  0.0 150.2 jit_solution(5249773133756344107)
XLA Ops:
  0.6 1.5 %shard_map.85 = (bf16[16,192,128]{2,1,0:T(8,128)(2,1)S(1)}, f32[1,192]{1,0:T(1,128)S(1)}) custom-call(s32[1,96]{1,0:T(1,128)} %bitcast.4, bf16[768,512]{1,0:T(8,128)(2,1)} %bitcast.3), custom_call_target="tpu_custom_call" | custom-call | tf_op jit(solution)/shard_map/pallas_call | solution.py:219
  2.2 25.4 %all_to_all.25.pieces = bf16[16,192,128]{2,1,0:T(8,128)(2,1)S(1)} all-to-all(bf16[16,192,128]{2,1,0:T(8,128)(2,1)S(1)} %get-tuple-element.12), channel_id=1, replica_groups=mesh['replica'=16,'owner'=64] {'replica'}, dimensions={0} | all-to-all | bytes 1572864 | tf_op jit(solution)/shard_map/all_to_all | solution.py:246
  27.6 0.0 copy-start
  27.6 0.3 shard_map.86
  27.9 50.0 %all_to_all.26 = bf16[64,2,256]{2,1,0:T(2,128)(2,1)S(1)} all-to-all(bf16[64,2,256]{2,1,0:T(2,128)(2,1)S(1)} %reshape.25), channel_id=1, replica_groups=mesh['replica'=16,'owner'=64] {'owner'}, dimensions={0} | all-to-all | bytes 131072 | tf_op jit(solution)/shard_map/all_to_all | solution.py:249
  77.9 0.0 copy-start.1
  78.0 0.1 shard_map.87
  78.1 19.9 %all_to_all.27.gathered = bf16[16,256,128]{2,1,0:T(8,128)(2,1)S(1)} all-to-all(bf16[16,256,128]{2,1,0:T(8,128)(2,1)S(1)} %shard_map.87), channel_id=1, replica_groups=mesh['replica'=16,'owner'=64] {'replica'}, dimensions={0} | all-to-all | bytes 2097152 | tf_op jit(solution)/shard_map/all_to_all | solution.py:251
  98.0 0.0 copy-done
  98.0 0.0 copy-done.1
  98.0 3.9 %shard_map.88 = (bf16[128,256]{1,0:T(8,128)(2,1)S(1)}, bf16[2,512,512]{2,1,0:T(8,128)(2,1)}, bf16[2,512,512]{2,1,0:T(8,128)(2,1)}, bf16[2,512,512]{2,1,0:T(8,128)(2,1)S(1)}) custom-call(bf16[16,256,128]{2,1,0:T(8,128)(2,1)S(1)} %all_to_all.27.gathered, f32[2,512,512]{2,1,0:T(8,128)S(1)} %copy-done, f32[2,512,512]{2,1,0:T(8,128)S(1)} %copy-done.1, ...), custom_call_target="tpu_custom_call" | custom-call | tf_op jit(solution)/shard_map/pallas_call | solution.py:219
  102.0 30.2 %all_to_all.28 = bf16[64,2,256]{2,1,0:T(2,128)(2,1)S(1)} all-to-all(bf16[64,2,256]{2,1,0:T(2,128)(2,1)S(1)} %reshape.27), channel_id=1, replica_groups=mesh['replica'=16,'owner'=64] {'owner'}, dimensions={0} | all-to-all | bytes 131072 | tf_op jit(solution)/shard_map/all_to_all | solution.py:262
  132.3 0.3 shard_map.89
  132.6 16.3 %all_to_all.29.pieces = bf16[16,192,128]{2,1,0:T(8,128)(2,1)S(1)} all-to-all(bf16[16,192,128]{2,1,0:T(8,128)(2,1)S(1)} %shard_map.89), channel_id=1, replica_groups=mesh['replica'=16,'owner'=64] {'replica'}, dimensions={0} | all-to-all | bytes 1572864 | tf_op jit(solution)/shard_map/all_to_all | solution.py:268
  148.9 1.3 shard_map.90
  (4 shorter events, 0.1 us)
Async XLA Ops:
  27.6 70.5 %copy-start = (f32[2,512,512]{2,1,0:T(8,128)S(1)}, f32[2,512,512]{2,1,0:T(8,128)}, u32[]{:S(2)}) copy-start(f32[2,512,512]{2,1,0:T(8,128)} %left.1) | copy-start | bytes 6291460
  77.9 20.1 %copy-start.1 = (f32[2,512,512]{2,1,0:T(8,128)S(1)}, f32[2,512,512]{2,1,0:T(8,128)}, u32[]{:S(2)}) copy-start(f32[2,512,512]{2,1,0:T(8,128)} %right.1) | copy-start | bytes 6291460

commit v5 on v4

--- a/solution.py
+++ b/solution.py
@@ -25,6 +25,11 @@
 
 def dot(a, b):
     return jnp.dot(a, b, preferred_element_type=f32)
+
+
+def split(a):
+    high = a.astype(bf16)
+    return high, (a - high.astype(f32)).astype(bf16)
 
 
 def permutation(dtype):
@@ -125,27 +130,29 @@
 
 def step_kernel(
     gathered, left, right, first_old, second_old, piece, first_new, second_new, last_new,
-    first_held, second_held, new, rows, sems, out_sems,
+    second_held, new, rows, sems, out_sems,
 ):
     loads = []
     for level in range(2):
-        for k, (old, held) in enumerate([(first_old, first_held), (second_old, second_held)]):
+        for k, (old, held) in enumerate([(second_old, second_held)]):
             loads.append(pltpu.make_async_copy(old.at[level], held.at[level], sems.at[level, k]))
             loads[-1].start()
     replica = lax.axis_index("replica")
     pair, tile = lax.shift_right_logical(replica, 2), replica & 3
     perm = permutation(bf16)
+    perm2 = jnp.concatenate([perm, perm], axis=1)
     for level in range(2):
         parts = [
-            dot(perm, left[level, g * 128 : (g + 1) * 128, :].astype(bf16)) for g in range(PAIRS)
+            dot(perm2, jnp.concatenate(split(left[level, g * 128 : (g + 1) * 128, :]), axis=0))
+            for g in range(PAIRS)
         ]
         turned = []
         for k in range(PAIRS):
             here = jnp.concatenate([part[k * 32 : (k + 1) * 32] for part in parts], axis=0)
             rows[level, k * 128 : (k + 1) * 128, :] = here.astype(bf16)
-            turned.append(here.T.astype(bf16))
-        left_t = jnp.concatenate(turned, axis=1)
-        right_b = right[level].astype(bf16)
+            turned.append(here.T)
+        left_high, left_low = split(jnp.concatenate(turned, axis=1))
+        right_high, right_low = split(right[level])
         grad = jnp.concatenate(
             [
                 jnp.concatenate(
@@ -159,10 +166,12 @@
             ],
             axis=0,
         )
-        rotated = dot(dot(left_t, grad).astype(bf16), right_b)
-        loads[2 * level].wait()
-        loads[2 * level + 1].wait()
-        first = beta_first * first_held[level].astype(f32) + (1.0 - beta_first) * rotated
+        half_high, half_low = split(dot(left_high, grad) + dot(left_low, grad))
+        rotated = dot(half_high, right_high) + (
+            dot(half_high, right_low) + dot(half_low, right_high)
+        )
+        loads[level].wait()
+        first = beta_first * first_old[level].astype(f32) + (1.0 - beta_first) * rotated
         second = beta_second * second_held[level].astype(f32) + (
             (1.0 - beta_second) * rotated
         ) * rotated
@@ -253,10 +262,10 @@
     piece, first, second, last_new = call(
         step_kernel,
         [shape((128, 2 * LANES), bf16), in_place, in_place, held],
-        (gathered, left_basis, right_basis, in_hbm(first_moment), in_hbm(second_moment)),
-        specs=[VMEM] * 3 + [HBM] * 2,
+        (gathered, left_basis, right_basis, first_moment, in_hbm(second_moment)),
+        specs=[VMEM] * 4 + [HBM],
         outs=[VMEM, HBM, HBM, VMEM],
-        scratch=[held] * 4 + [pltpu.SemaphoreType.DMA((2, 2)), pltpu.SemaphoreType.DMA((2,))],
+        scratch=[held] * 3 + [pltpu.SemaphoreType.DMA((2, 1)), pltpu.SemaphoreType.DMA((2,))],
         limit=16,
     )
     returned = lax.all_to_all(piece.reshape(64, 2, 2 * LANES), "owner", 0, 0)

time: 151 us -> 153 us (1.013)
  no operation moved by 1% of the time
where the time goes in v5:
time: 153 us
  blocking collectives  142 us (93%)
  Pallas kernels  8.86 us (6%)
    all_to_all x1, blocking collectives, local(): lax.all_to_all(placed.reshape(64, 2, 2 * LANES), 'owner', 0, 0)  50 us
    all_to_all x1, blocking collectives, local(): returned = lax.all_to_all(piece.reshape(64, 2, 2 * LANES), 'owner', 0, 0)  30.4 us
    all_to_all x1, blocking collectives, local(): parts = lax.all_to_all(pieces, 'replica', 0, 0)  25.5 us
    all_to_all x1, blocking collectives, local(): gathered = lax.all_to_all(copies, 'replica', 0, 0)  19.9 us
    all_to_all x1, blocking collectives, local(): joined = lax.all_to_all(copies, 'replica', 0, 0)  16.3 us
    pallas_call x6, Pallas kernels, call(): pl.pallas_call(kernel, out_shape=out, in_specs=specs or [VMEM] * len(inpu...  8.86 us

profile of v5, /device:TPU:8, one launch (start us, length us, event | category | flops | bytes accessed | tf_op | source)
XLA Modules:
  0.0 152.9 jit_solution(1098204399157197537)
XLA Ops:
  0.6 1.5 shard_map.85
  2.2 0.0 copy-start.2
  2.2 25.5 %all_to_all.25.pieces = bf16[16,192,128]{2,1,0:T(8,128)(2,1)S(1)} all-to-all(bf16[16,192,128]{2,1,0:T(8,128)(2,1)S(1)} %get-tuple-element.12), channel_id=1, replica_groups=mesh['replica'=16,'owner'=64] {'replica'}, dimensions={0} | all-to-all | bytes 1572864 | tf_op jit(solution)/shard_map/all_to_all | solution.py:255
  27.7 0.0 copy-start
  27.7 0.3 shard_map.86
  28.0 50.0 %all_to_all.26 = bf16[64,2,256]{2,1,0:T(2,128)(2,1)S(1)} all-to-all(bf16[64,2,256]{2,1,0:T(2,128)(2,1)S(1)} %reshape.25), channel_id=1, replica_groups=mesh['replica'=16,'owner'=64] {'owner'}, dimensions={0} | all-to-all | bytes 131072 | tf_op jit(solution)/shard_map/all_to_all | solution.py:258
  78.1 0.0 copy-start.1
  78.1 0.1 shard_map.87
  78.2 19.9 %all_to_all.27.gathered = bf16[16,256,128]{2,1,0:T(8,128)(2,1)S(1)} all-to-all(bf16[16,256,128]{2,1,0:T(8,128)(2,1)S(1)} %shard_map.87), channel_id=1, replica_groups=mesh['replica'=16,'owner'=64] {'replica'}, dimensions={0} | all-to-all | bytes 2097152 | tf_op jit(solution)/shard_map/all_to_all | solution.py:260
  98.2 0.0 copy-done.2
  98.2 0.0 copy-done
  98.2 0.0 copy-done.1
  98.2 5.4 %shard_map.88 = (bf16[128,256]{1,0:T(8,128)(2,1)S(1)}, bf16[2,512,512]{2,1,0:T(8,128)(2,1)}, bf16[2,512,512]{2,1,0:T(8,128)(2,1)}, bf16[2,512,512]{2,1,0:T(8,128)(2,1)S(1)}) custom-call(bf16[16,256,128]{2,1,0:T(8,128)(2,1)S(1)} %all_to_all.27.gathered, f32[2,512,512]{2,1,0:T(8,128)S(1)} %copy-done, f32[2,512,512]{2,1,0:T(8,128)S(1)} %copy-done.1, ...), custom_call_target="tpu_custom_call" | custom-call | tf_op jit(solution)/shard_map/pallas_call | solution.py:228
  103.6 0.0 copy-start.3
  103.6 1.0 copy-done.3
  104.5 0.0 copy-start.4
  104.6 30.4 %all_to_all.28 = bf16[64,2,256]{2,1,0:T(2,128)(2,1)S(1)} all-to-all(bf16[64,2,256]{2,1,0:T(2,128)(2,1)S(1)} %reshape.27), channel_id=1, replica_groups=mesh['replica'=16,'owner'=64] {'owner'}, dimensions={0} | all-to-all | bytes 131072 | tf_op jit(solution)/shard_map/all_to_all | solution.py:271
  135.0 0.3 shard_map.89
  135.2 16.3 %all_to_all.29.pieces = bf16[16,192,128]{2,1,0:T(8,128)(2,1)S(1)} all-to-all(bf16[16,192,128]{2,1,0:T(8,128)(2,1)S(1)} %shard_map.89), channel_id=1, replica_groups=mesh['replica'=16,'owner'=64] {'replica'}, dimensions={0} | all-to-all | bytes 1572864 | tf_op jit(solution)/shard_map/all_to_all | solution.py:277
  151.6 0.0 copy-done.4
  151.6 1.3 shard_map.90
  (4 shorter events, 0.1 us)
Async XLA Ops:
  2.2 96.0 %copy-start.2 = (bf16[2,512,512]{2,1,0:T(8,128)(2,1)S(1)}, bf16[2,512,512]{2,1,0:T(8,128)(2,1)}, u32[]{:S(2)}) copy-start(bf16[2,512,512]{2,1,0:T(8,128)(2,1)} %first_old.1) | copy-start | bytes 3145732
  27.7 70.5 %copy-start = (f32[2,512,512]{2,1,0:T(8,128)S(1)}, f32[2,512,512]{2,1,0:T(8,128)}, u32[]{:S(2)}) copy-start(f32[2,512,512]{2,1,0:T(8,128)} %left.1) | copy-start | bytes 6291460
  78.1 20.1 %copy-start.1 = (f32[2,512,512]{2,1,0:T(8,128)S(1)}, f32[2,512,512]{2,1,0:T(8,128)}, u32[]{:S(2)}) copy-start(f32[2,512,512]{2,1,0:T(8,128)} %right.1) | copy-start | bytes 6291460
  103.6 1.0 copy-start.3
  104.5 47.0 %copy-start.4 = (bf16[2,512,512]{2,1,0:T(8,128)(2,1)S(1)}, bf16[2,512,512]{2,1,0:T(8,128)(2,1)}, u32[]{:S(2)}) copy-start(bf16[2,512,512]{2,1,0:T(8,128)(2,1)} %copy-done.3) | copy-start | bytes 3145732

commit v6 on v4

--- a/solution.py
+++ b/solution.py
@@ -25,6 +25,15 @@
 
 def dot(a, b):
     return jnp.dot(a, b, preferred_element_type=f32)
+
+
+def dot_t(a, b):
+    return lax.dot_general(a, b, (((0,), (0,)), ((), ())), preferred_element_type=f32)
+
+
+def split(a):
+    high = a.astype(bf16)
+    return high, (a - high.astype(f32)).astype(bf16)
 
 
 def permutation(dtype):
@@ -125,7 +134,7 @@
 
 def step_kernel(
     gathered, left, right, first_old, second_old, piece, first_new, second_new, last_new,
-    first_held, second_held, new, rows, sems, out_sems,
+    first_held, second_held, new, sems, out_sems,
 ):
     loads = []
     for level in range(2):
@@ -134,32 +143,43 @@
             loads[-1].start()
     replica = lax.axis_index("replica")
     pair, tile = lax.shift_right_logical(replica, 2), replica & 3
-    perm = permutation(bf16)
+    perm = inverse_permutation(bf16)
+    out = lax.broadcasted_iota(jnp.int32, (2 * GROUP, 8 * GROUP), 0)
+    src = lax.broadcasted_iota(jnp.int32, (2 * GROUP, 8 * GROUP), 1)
+    mine_of = (src == (out >> 1) * 8 + pair * 2 + (out & 1)).astype(bf16)
     for level in range(2):
-        parts = [
-            dot(perm, left[level, g * 128 : (g + 1) * 128, :].astype(bf16)) for g in range(PAIRS)
-        ]
-        turned = []
-        for k in range(PAIRS):
-            here = jnp.concatenate([part[k * 32 : (k + 1) * 32] for part in parts], axis=0)
-            rows[level, k * 128 : (k + 1) * 128, :] = here.astype(bf16)
-            turned.append(here.T.astype(bf16))
-        left_t = jnp.concatenate(turned, axis=1)
-        right_b = right[level].astype(bf16)
         grad = jnp.concatenate(
             [
-                jnp.concatenate(
-                    [
-                        gathered[k * TILES + t, level * 128 : (level + 1) * 128, :]
-                        for t in range(TILES)
-                    ],
-                    axis=1,
-                )
-                for k in range(PAIRS)
+                dot(
+                    perm,
+                    jnp.concatenate(
+                        [
+                            jnp.concatenate(
+                                [
+                                    gathered[
+                                        k * TILES + t,
+                                        level * 128 + g * 32 : level * 128 + (g + 1) * 32,
+                                        :,
+                                    ]
+                                    for t in range(TILES)
+                                ],
+                                axis=1,
+                            )
+                            for k in range(PAIRS)
+                        ],
+                        axis=0,
+                    ),
+                ).astype(bf16)
+                for g in range(PAIRS)
             ],
             axis=0,
         )
-        rotated = dot(dot(left_t, grad).astype(bf16), right_b)
+        left_high, left_low = split(left[level])
+        right_high, right_low = split(right[level])
+        half_high, half_low = split(dot_t(left_high, grad) + dot_t(left_low, grad))
+        rotated = dot(half_high, right_high) + (
+            dot(half_high, right_low) + dot(half_low, right_high)
+        )
         loads[2 * level].wait()
         loads[2 * level + 1].wait()
         first = beta_first * first_held[level].astype(f32) + (1.0 - beta_first) * rotated
@@ -178,7 +198,9 @@
                 store.start()
         scaled = second * (1.0 / bias_second)
         update = (first * (1.0 / bias_first)) / (scaled * lax.rsqrt(scaled) + epsilon)
-        mine = rows[level, pl.ds(pl.multiple_of(pair * 128, 128), 128), :]
+        mine = jnp.concatenate(
+            [dot(mine_of, left_high[g * 128 : (g + 1) * 128]) for g in range(PAIRS)], axis=0
+        ).astype(bf16)
         left_half = dot(mine, update.astype(bf16)).astype(bf16)
         back = right[level, pl.ds(pl.multiple_of(tile * LANES, LANES), LANES), :].astype(bf16)
         piece[:, level * LANES : (level + 1) * LANES] = lax.dot_general(
@@ -256,7 +278,7 @@
         (gathered, left_basis, right_basis, in_hbm(first_moment), in_hbm(second_moment)),
         specs=[VMEM] * 3 + [HBM] * 2,
         outs=[VMEM, HBM, HBM, VMEM],
-        scratch=[held] * 4 + [pltpu.SemaphoreType.DMA((2, 2)), pltpu.SemaphoreType.DMA((2,))],
+        scratch=[held] * 3 + [pltpu.SemaphoreType.DMA((2, 2)), pltpu.SemaphoreType.DMA((2,))],
         limit=16,
     )
     returned = lax.all_to_all(piece.reshape(64, 2, 2 * LANES), "owner", 0, 0)

time: 151 us -> 152 us (level)
  no operation moved by 1% of the time
where the time goes in v6:
time: 152 us; the launch traced here: 151 us
  blocking collectives  142 us (93%)
  Pallas kernels  8.71 us (6%)
    all_to_all x1, blocking collectives, local(): lax.all_to_all(placed.reshape(64, 2, 2 * LANES), 'owner', 0, 0)  50 us
    all_to_all x1, blocking collectives, local(): returned = lax.all_to_all(piece.reshape(64, 2, 2 * LANES), 'owner', 0, 0)  30.2 us
    all_to_all x1, blocking collectives, local(): parts = lax.all_to_all(pieces, 'replica', 0, 0)  25.4 us
    all_to_all x1, blocking collectives, local(): gathered = lax.all_to_all(copies, 'replica', 0, 0)  19.9 us
    all_to_all x1, blocking collectives, local(): joined = lax.all_to_all(copies, 'replica', 0, 0)  16.3 us
    pallas_call x6, Pallas kernels, call(): pl.pallas_call(kernel, out_shape=out, in_specs=specs or [VMEM] * len(inpu...  8.71 us

profile of v6, /device:TPU:8, one launch (start us, length us, event | category | flops | bytes accessed | tf_op | source)
XLA Modules:
  0.0 151.5 jit_solution(15360185249933849071)
XLA Ops:
  0.6 1.5 %shard_map.85 = (bf16[16,192,128]{2,1,0:T(8,128)(2,1)S(1)}, f32[1,192]{1,0:T(1,128)S(1)}) custom-call(s32[1,96]{1,0:T(1,128)} %bitcast.4, bf16[768,512]{1,0:T(8,128)(2,1)} %bitcast.3), custom_call_target="tpu_custom_call" | custom-call | tf_op jit(solution)/shard_map/pallas_call | solution.py:241
  2.2 25.4 %all_to_all.25.pieces = bf16[16,192,128]{2,1,0:T(8,128)(2,1)S(1)} all-to-all(bf16[16,192,128]{2,1,0:T(8,128)(2,1)S(1)} %get-tuple-element.12), channel_id=1, replica_groups=mesh['replica'=16,'owner'=64] {'replica'}, dimensions={0} | all-to-all | bytes 1572864 | tf_op jit(solution)/shard_map/all_to_all | solution.py:268
  27.6 0.0 copy-start
  27.6 0.3 shard_map.86
  27.9 50.0 %all_to_all.26 = bf16[64,2,256]{2,1,0:T(2,128)(2,1)S(1)} all-to-all(bf16[64,2,256]{2,1,0:T(2,128)(2,1)S(1)} %reshape.25), channel_id=1, replica_groups=mesh['replica'=16,'owner'=64] {'owner'}, dimensions={0} | all-to-all | bytes 131072 | tf_op jit(solution)/shard_map/all_to_all | solution.py:271
  77.9 0.0 copy-start.1
  78.0 0.1 shard_map.87
  78.1 19.9 %all_to_all.27.gathered = bf16[16,256,128]{2,1,0:T(8,128)(2,1)S(1)} all-to-all(bf16[16,256,128]{2,1,0:T(8,128)(2,1)S(1)} %shard_map.87), channel_id=1, replica_groups=mesh['replica'=16,'owner'=64] {'replica'}, dimensions={0} | all-to-all | bytes 2097152 | tf_op jit(solution)/shard_map/all_to_all | solution.py:273
  98.0 0.0 copy-done
  98.0 0.0 copy-done.1
  98.0 5.2 %shard_map.88 = (bf16[128,256]{1,0:T(8,128)(2,1)S(1)}, bf16[2,512,512]{2,1,0:T(8,128)(2,1)}, bf16[2,512,512]{2,1,0:T(8,128)(2,1)}, bf16[2,512,512]{2,1,0:T(8,128)(2,1)S(1)}) custom-call(bf16[16,256,128]{2,1,0:T(8,128)(2,1)S(1)} %all_to_all.27.gathered, f32[2,512,512]{2,1,0:T(8,128)S(1)} %copy-done, f32[2,512,512]{2,1,0:T(8,128)S(1)} %copy-done.1, ...), custom_call_target="tpu_custom_call" | custom-call | tf_op jit(solution)/shard_map/pallas_call | solution.py:241
  103.3 30.2 %all_to_all.28 = bf16[64,2,256]{2,1,0:T(2,128)(2,1)S(1)} all-to-all(bf16[64,2,256]{2,1,0:T(2,128)(2,1)S(1)} %reshape.27), channel_id=1, replica_groups=mesh['replica'=16,'owner'=64] {'owner'}, dimensions={0} | all-to-all | bytes 131072 | tf_op jit(solution)/shard_map/all_to_all | solution.py:284
  133.6 0.3 shard_map.89
  133.9 16.3 %all_to_all.29.pieces = bf16[16,192,128]{2,1,0:T(8,128)(2,1)S(1)} all-to-all(bf16[16,192,128]{2,1,0:T(8,128)(2,1)S(1)} %shard_map.89), channel_id=1, replica_groups=mesh['replica'=16,'owner'=64] {'replica'}, dimensions={0} | all-to-all | bytes 1572864 | tf_op jit(solution)/shard_map/all_to_all | solution.py:290
  150.2 1.3 shard_map.90
  (4 shorter events, 0.1 us)
Async XLA Ops:
  27.6 70.5 %copy-start = (f32[2,512,512]{2,1,0:T(8,128)S(1)}, f32[2,512,512]{2,1,0:T(8,128)}, u32[]{:S(2)}) copy-start(f32[2,512,512]{2,1,0:T(8,128)} %left.1) | copy-start | bytes 6291460
  77.9 20.1 %copy-start.1 = (f32[2,512,512]{2,1,0:T(8,128)S(1)}, f32[2,512,512]{2,1,0:T(8,128)}, u32[]{:S(2)}) copy-start(f32[2,512,512]{2,1,0:T(8,128)} %right.1) | copy-start | bytes 6291460

commit v7 on v6

--- a/solution.py
+++ b/solution.py
@@ -196,8 +196,8 @@
             ]
             for store in stores:
                 store.start()
-        scaled = second * (1.0 / bias_second)
-        update = (first * (1.0 / bias_first)) / (scaled * lax.rsqrt(scaled) + epsilon)
+        root = second * lax.rsqrt(second)
+        update = first / (root * (bias_first / bias_second**0.5) + bias_first * epsilon)
         mine = jnp.concatenate(
             [dot(mine_of, left_high[g * 128 : (g + 1) * 128]) for g in range(PAIRS)], axis=0
         ).astype(bf16)

time: 152 us -> 152 us (level)
  no operation moved by 1% of the time
where the time goes in v7:
time: 152 us; the launch traced here: 151 us
  blocking collectives  142 us (93%)
  Pallas kernels  8.63 us (6%)
    all_to_all x1, blocking collectives, local(): lax.all_to_all(placed.reshape(64, 2, 2 * LANES), 'owner', 0, 0)  50 us
    all_to_all x1, blocking collectives, local(): returned = lax.all_to_all(piece.reshape(64, 2, 2 * LANES), 'owner', 0, 0)  30.2 us
    all_to_all x1, blocking collectives, local(): parts = lax.all_to_all(pieces, 'replica', 0, 0)  25.4 us
    all_to_all x1, blocking collectives, local(): gathered = lax.all_to_all(copies, 'replica', 0, 0)  19.9 us
    all_to_all x1, blocking collectives, local(): joined = lax.all_to_all(copies, 'replica', 0, 0)  16.3 us
    pallas_call x6, Pallas kernels, call(): pl.pallas_call(kernel, out_shape=out, in_specs=specs or [VMEM] * len(inpu...  8.63 us

profile of v7, /device:TPU:8, one launch (start us, length us, event | category | flops | bytes accessed | tf_op | source)
XLA Modules:
  0.0 151.4 jit_solution(15461842466737178122)
XLA Ops:
  0.6 1.5 %shard_map.85 = (bf16[16,192,128]{2,1,0:T(8,128)(2,1)S(1)}, f32[1,192]{1,0:T(1,128)S(1)}) custom-call(s32[1,96]{1,0:T(1,128)} %bitcast.4, bf16[768,512]{1,0:T(8,128)(2,1)} %bitcast.3), custom_call_target="tpu_custom_call" | custom-call | tf_op jit(solution)/shard_map/pallas_call | solution.py:241
  2.2 25.4 %all_to_all.25.pieces = bf16[16,192,128]{2,1,0:T(8,128)(2,1)S(1)} all-to-all(bf16[16,192,128]{2,1,0:T(8,128)(2,1)S(1)} %get-tuple-element.12), channel_id=1, replica_groups=mesh['replica'=16,'owner'=64] {'replica'}, dimensions={0} | all-to-all | bytes 1572864 | tf_op jit(solution)/shard_map/all_to_all | solution.py:268
  27.6 0.0 copy-start
  27.6 0.3 shard_map.86
  27.9 50.0 %all_to_all.26 = bf16[64,2,256]{2,1,0:T(2,128)(2,1)S(1)} all-to-all(bf16[64,2,256]{2,1,0:T(2,128)(2,1)S(1)} %reshape.25), channel_id=1, replica_groups=mesh['replica'=16,'owner'=64] {'owner'}, dimensions={0} | all-to-all | bytes 131072 | tf_op jit(solution)/shard_map/all_to_all | solution.py:271
  77.9 0.0 copy-start.1
  78.0 0.1 shard_map.87
  78.1 19.9 %all_to_all.27.gathered = bf16[16,256,128]{2,1,0:T(8,128)(2,1)S(1)} all-to-all(bf16[16,256,128]{2,1,0:T(8,128)(2,1)S(1)} %shard_map.87), channel_id=1, replica_groups=mesh['replica'=16,'owner'=64] {'replica'}, dimensions={0} | all-to-all | bytes 2097152 | tf_op jit(solution)/shard_map/all_to_all | solution.py:273
  98.0 0.0 copy-done
  98.0 0.0 copy-done.1
  98.0 5.1 %shard_map.88 = (bf16[128,256]{1,0:T(8,128)(2,1)S(1)}, bf16[2,512,512]{2,1,0:T(8,128)(2,1)}, bf16[2,512,512]{2,1,0:T(8,128)(2,1)}, bf16[2,512,512]{2,1,0:T(8,128)(2,1)S(1)}) custom-call(bf16[16,256,128]{2,1,0:T(8,128)(2,1)S(1)} %all_to_all.27.gathered, f32[2,512,512]{2,1,0:T(8,128)S(1)} %copy-done, f32[2,512,512]{2,1,0:T(8,128)S(1)} %copy-done.1, ...), custom_call_target="tpu_custom_call" | custom-call | tf_op jit(solution)/shard_map/pallas_call | solution.py:241
  103.2 30.2 %all_to_all.28 = bf16[64,2,256]{2,1,0:T(2,128)(2,1)S(1)} all-to-all(bf16[64,2,256]{2,1,0:T(2,128)(2,1)S(1)} %reshape.27), channel_id=1, replica_groups=mesh['replica'=16,'owner'=64] {'owner'}, dimensions={0} | all-to-all | bytes 131072 | tf_op jit(solution)/shard_map/all_to_all | solution.py:284
  133.5 0.3 shard_map.89
  133.8 16.3 %all_to_all.29.pieces = bf16[16,192,128]{2,1,0:T(8,128)(2,1)S(1)} all-to-all(bf16[16,192,128]{2,1,0:T(8,128)(2,1)S(1)} %shard_map.89), channel_id=1, replica_groups=mesh['replica'=16,'owner'=64] {'replica'}, dimensions={0} | all-to-all | bytes 1572864 | tf_op jit(solution)/shard_map/all_to_all | solution.py:290
  150.1 1.3 shard_map.90
  (4 shorter events, 0.1 us)
Async XLA Ops:
  27.6 70.5 %copy-start = (f32[2,512,512]{2,1,0:T(8,128)S(1)}, f32[2,512,512]{2,1,0:T(8,128)}, u32[]{:S(2)}) copy-start(f32[2,512,512]{2,1,0:T(8,128)} %left.1) | copy-start | bytes 6291460
  77.9 20.1 %copy-start.1 = (f32[2,512,512]{2,1,0:T(8,128)S(1)}, f32[2,512,512]{2,1,0:T(8,128)}, u32[]{:S(2)}) copy-start(f32[2,512,512]{2,1,0:T(8,128)} %right.1) | copy-start | bytes 6291460
